TPU v7x, 32 devices: a whole 2x2x4 slice. The times are simulated.
32 devices in a mesh: scene: 2 (over x), space: 8 (over z, y), sub: 2 (over core).
Axes of the slice: x: 2, y: 2, z: 4, core: 2. Of those that a mesh axis runs over, the one named last changes fastest.
Arguments:
- features: bfloat16 [64, 64, 512], P(('scene', 'space', 'sub')), parts along dimension 0, may hold values from -6 to 6
- occupancy: int32 [64, 512], P(('scene', 'space', 'sub')), parts along dimension 0, may hold values 0 or 1
- face_owner: int32 [64, 6, 1], P(('scene', 'space', 'sub')), parts along dimension 0, may hold values from 0 to 15; in each aligned block of 12 rows (0 to 11, 12 to 23, ..., all dimensions but the last counted through in order) at most 2 rows name the same one
- face_slot: int32 [64, 6], P(('scene', 'space', 'sub')), parts along dimension 0, may hold values from 0 to 1
- line_owner: int32 [64, 20, 1], P(('scene', 'space', 'sub')), parts along dimension 0, may hold values from 0 to 15; in each aligned block of 40 rows (0 to 39, 40 to 79, ..., all dimensions but the last counted through in order) at most 4 rows name the same one
- line_slot: int32 [64, 20], P(('scene', 'space', 'sub')), parts along dimension 0, may hold values from 0 to 1
- weight_one: bfloat16 [27, 64, 64], replicated, may hold values from -0.15625 to 0.15625
- weight_two: bfloat16 [27, 64, 64], replicated, may hold values from -0.15625 to 0.15625
- cotangent: bfloat16 [64, 64, 512], P(('scene', 'space', 'sub')), parts along dimension 0, may hold values from -6 to 6
Outputs:
- block_out: bfloat16 [64, 64, 512], P(('scene', 'space', 'sub')), parts along dimension 0
- feature_grad: bfloat16 [64, 64, 512], P(('scene', 'space', 'sub')), parts along dimension 0
- first_grad: float32 [54, 64, 64], P('scene'), parts along dimension 0
- second_grad: float32 [54, 64, 64], P('scene'), parts along dimension 0
There are 2 independent parts, one for each index of `scene`. A program takes and returns all parts, laid end to end along the dimension named above; an argument that names none is the same for every part. Nothing has to cross between parts.
Inputs may be any that keep to these rules, and one draw needn't show every extreme that they name: `face_owner`: owners are numbered along space+sub. Among the 12 entries of one owner's tiles no owner is named more than 2 times, and in some owner's tiles one owner is named exactly 2 times. `line_owner`: owners are numbered along space+sub. Among the 40 entries of one owner's tiles no owner is named more than 4 times, and in some owner's tiles one owner is named exactly 4 times.
All inputs are finite; a program needn't handle non-finite values. No bound on the sum of `occupancy` on one device may be relied on, other than what follows from the above.
Results may differ from a plain program's by a relative error of at most 0.0032.
Values may be sent and summed in bfloat16 or wider, within the bound.
A program may use at most 128 MiB of HBM per device.

v0:
```python
import math

import jax
import jax.numpy as jnp
from jax import lax
from jax.experimental import pallas as pl
from jax.experimental.pallas import tpu as pltpu
from jax.sharding import PartitionSpec as P

F32 = jnp.float32
BF16 = jnp.bfloat16
OWNER_AXES = ("space", "sub")

_VECTORS = [(x, y, z) for x in (-1, 0, 1) for y in (-1, 0, 1) for z in (-1, 0, 1)]
EXTRA = [v for v in _VECTORS if sum(c != 0 for c in v) == 2]
EXTRA = EXTRA + [v for v in _VECTORS if sum(c != 0 for c in v) == 3]
OPPOSITE = (1, 0, 3, 2, 5, 4)


def line_need():
    need = []
    for vector in EXTRA:
        zero = [a for a in range(3) if vector[a] == 0]
        main = zero[0] if zero else 2
        rest = [a for a in range(3) if a != main]
        b1 = 0 if vector[rest[0]] > 0 else 1
        b2 = 0 if vector[rest[1]] > 0 else 1
        need.append(main * 4 + b1 * 2 + b2)
    return need


DEAL = [k for k in range(27) if k % 3 < 2] + [k for k in range(27) if k % 3 == 2]


def cut_pieces(values, tile, faces, lines):
    for f in range(6):
        end = 7 * (f % 2)
        if f // 2 == 0:
            piece = values[end]
        elif f // 2 == 1:
            piece = values[:, end]
        else:
            piece = values[:, :, end, :]
        faces[tile * 6 + f] = piece
    for main in range(3):
        for b1 in range(2):
            for b2 in range(2):
                if main == 2:
                    piece = values[7 * b1, 7 * b2]
                elif main == 1:
                    piece = values[7 * b1, :, 7 * b2, :]
                else:
                    piece = values[:, 7 * b1, 7 * b2, :]
                lines[tile * 12 + main * 4 + b1 * 2 + b2] = piece


def conv_back(up_rows, weight, wide, spread, tile, own, grad_faces, grad_lines):
    c = up_rows.shape[-1]
    cube = up_rows.reshape(8, 8, 8, c)
    for j in range(3):
        wide[2:10, j : j + 8, :, j * c : (j + 1) * c] = cube
    total = None
    for kx in range(3):
        cols = wide[2 - kx : 12 - kx].reshape(800, 4 * c).astype(BF16)
        term = jnp.dot(cols, weight[kx * 4 * c : (kx + 1) * 4 * c, :], preferred_element_type=F32)
        total = term if total is None else total + term
    total = total.reshape(10, 10, 8, 3 * c)
    spread[:, :, 16:24, :] = jnp.zeros((10, 10, 8, c), F32)
    spread[:, :, 8:16, :] = total[:, :, :, :c]
    spread[:, :, 9:17, :] += total[:, :, :, c : 2 * c]
    spread[:, :, 10:18, :] += total[:, :, :, 2 * c :]
    own[tile] = spread[1:9, 1:9, 9:17, :].reshape(64, 8, c)
    for f in range(6):
        end = 9 * (f % 2)
        if f // 2 == 0:
            piece = spread[end, 1:9, 9:17, :]
        elif f // 2 == 1:
            piece = spread[1:9, end, 9:17, :]
        else:
            piece = spread[1:9, 1:9, 8 + end, :]
        grad_faces[tile * 6 + f] = piece
    for e, vector in enumerate(EXTRA):
        px, py, pz = [9 if d > 0 else 0 for d in vector]
        if vector[2] == 0:
            piece = spread[px, py, 9:17, :]
        elif vector[1] == 0:
            piece = spread[px, 1:9, 8 + pz, :]
        elif vector[0] == 0:
            piece = spread[1:9, py, 8 + pz, :]
        else:
            row = spread[px, py, 8 + pz : 9 + pz, :]
            spot = 0 if vector[2] > 0 else 7
            at = lax.broadcasted_iota(jnp.int32, (8, c), 0)
            piece = jnp.where(at == spot, jnp.broadcast_to(row, (8, c)), 0.0)
        grad_lines[tile * 20 + e] = piece


def fill_outgoing(idx, out, faces, lines, grad_faces, grad_lines):
    served_face, served_line, inv_face, inv_line = idx
    owners, fcap = served_face.shape
    lcap = served_line.shape[1]
    c = faces.shape[-1]

    def one(d, carry):
        rows = []
        for s in range(fcap):
            fwd = faces[served_face[d, s]].reshape(64, c)
            back = grad_faces[inv_face[d, s]].reshape(64, c)
            rows.append(jnp.concatenate([fwd, back], axis=1))
        for s in range(lcap):
            fwd = lines[served_line[d, s]]
            back = grad_lines[inv_line[d, s]]
            rows.append(jnp.concatenate([fwd, back], axis=1))
        out[d] = jnp.concatenate(rows, axis=0).astype(BF16)
        return carry

    lax.fori_loop(0, owners, one, 0)


def unpack(arrived, got_faces, got_lines, fcap, lcap):
    owners = arrived.shape[0]

    def one(d, carry):
        block = arrived[d].astype(F32)
        for s in range(fcap):
            got_faces[d * fcap + s] = block[s * 64 : (s + 1) * 64].reshape(8, 8, -1)
        base = fcap * 64
        for s in range(lcap):
            got_lines[d * lcap + s] = block[base + s * 8 : base + (s + 1) * 8]
        return carry

    lax.fori_loop(0, owners, one, 0)


def build_columns(cube, tile, face_pos, line_pos, got_faces, got_lines, block, wide, cols):
    c = cube.shape[-1]
    block[1:9, 1:9, 8:16, :] = cube
    for f in range(6):
        piece = got_faces[face_pos[tile * 6 + f]][:, :, :c]
        end = 9 * (f % 2)
        if f // 2 == 0:
            block[end, 1:9, 8:16, :] = piece
        elif f // 2 == 1:
            block[1:9, end, 8:16, :] = piece
        else:
            block[1:9, 1:9, 7 + end, :] = piece
    for e, vector in enumerate(EXTRA):
        piece = got_lines[line_pos[tile * 20 + e]][:, :c]
        px, py, pz = [9 if d > 0 else 0 for d in vector]
        if vector[2] == 0:
            block[px, py, 8:16, :] = piece
        elif vector[1] == 0:
            block[px, 1:9, 7 + pz, :] = piece
        elif vector[0] == 0:
            block[1:9, py, 7 + pz, :] = piece
        else:
            spot = 0 if vector[2] > 0 else 7
            block[px, py, 7 + pz : 8 + pz, :] = piece[spot : spot + 1]
    for kz in range(3):
        wide[:, :, :, kz * c : (kz + 1) * c] = block[:, :, 7 + kz : 15 + kz, :]
    for kxy in range(9):
        kx, ky = kxy // 3, kxy % 3
        window = wide[kx : kx + 8, ky : ky + 8].reshape(512, 4 * c).astype(BF16)
        cols[tile * 512 : (tile + 1) * 512, kxy * 4 * c : (kxy + 1) * 4 * c] = window


def fold_pieces(idx, got_faces, got_lines, face_sums, line_sums, own, tiles):
    served_face, served_line = idx
    owners, fcap = served_face.shape
    lcap = served_line.shape[1]
    c = own.shape[-1]
    face_sums[...] = jnp.zeros_like(face_sums)
    line_sums[...] = jnp.zeros_like(line_sums)

    def one(d, carry):
        for s in range(fcap):
            to = served_face[d, s]
            face_sums[to] = face_sums[to] + got_faces[d * fcap + s]
        for s in range(lcap):
            to = served_line[d, s]
            line_sums[to] = line_sums[to] + got_lines[d * lcap + s]
        return carry

    lax.fori_loop(0, owners, one, 0)
    for tile in range(tiles):
        for f in range(6):
            piece = face_sums[tile * 6 + f][:, :, c:]
            end = 7 * (f % 2)
            if f // 2 == 0:
                own[tile, end] += piece
            elif f // 2 == 1:
                own[tile, :, end] += piece
            else:
                own[tile, :, :, end, :] += piece
        for main in range(3):
            for b1 in range(2):
                for b2 in range(2):
                    piece = line_sums[tile * 12 + main * 4 + b1 * 2 + b2][:, c:]
                    if main == 2:
                        own[tile, 7 * b1, 7 * b2] += piece
                    elif main == 1:
                        own[tile, 7 * b1, :, 7 * b2, :] += piece
                    else:
                        own[tile, :, 7 * b1, 7 * b2, :] += piece


def deal_term(upstream, cols, terms):
    c = upstream.shape[0]
    term = jnp.dot(upstream, cols[...], preferred_element_type=F32)
    owners = terms.shape[0]
    share = terms.shape[2] // c
    for d in range(owners):
        parts = []
        for k in DEAL[d * share : (d + 1) * share]:
            lane = (k // 3) * 4 * c + (k % 3) * c
            parts.append(term[:, lane : lane + c])
        while len(parts) < share:
            parts.append(jnp.zeros((c, c), F32))
        terms[d] = (parts[0] if share == 1 else jnp.concatenate(parts, axis=1)).astype(BF16)


def first_kernel(sf, sl, vf, vl, feat, occ, cot, wb, out, rows, own,
                 faces, lines, grad_faces, grad_lines, wide, spread):
    tiles, c = feat.shape[0], feat.shape[1]
    wide[...] = jnp.zeros_like(wide)
    grad_faces[tiles * 6] = jnp.zeros((8, 8, c), F32)
    grad_lines[tiles * 20] = jnp.zeros((8, c), F32)
    for t in range(tiles):
        live = occ[t : t + 1, :].astype(F32)
        masked = (feat[t].astype(F32) * live).T
        rows[t] = masked.reshape(64, 8, c)
        cut_pieces(masked.reshape(8, 8, 8, c), t, faces, lines)
        upstream = (cot[t].astype(F32) * live).T
        conv_back(upstream, wb, wide, spread, t, own, grad_faces, grad_lines)
    fill_outgoing((sf, sl, vf, vl), out, faces, lines, grad_faces, grad_lines)


def second_kernel(sf, sl, vf, vl, fp, lp, arrived, rows, own_in, occ, wf, wb,
                  out, hidden_rows, own_out, terms,
                  faces, lines, grad_faces, grad_lines, wide_back, spread,
                  got_faces, got_lines, face_sums, line_sums, block, wide, cols, own):
    tiles, c = rows.shape[0], rows.shape[3]
    fcap, lcap = sf.shape[1], sl.shape[1]
    wide_back[...] = jnp.zeros_like(wide_back)
    wide[:, :, :, 3 * c :] = jnp.zeros((10, 10, 8, c), F32)
    grad_faces[tiles * 6] = jnp.zeros((8, 8, c), F32)
    grad_lines[tiles * 20] = jnp.zeros((8, c), F32)
    unpack(arrived, got_faces, got_lines, fcap, lcap)
    for t in range(tiles):
        own[t] = own_in[t].reshape(8, 8, 8, c)
        build_columns(rows[t].reshape(8, 8, 8, c), t, fp, lp, got_faces, got_lines, block, wide, cols)
    fold_pieces((sf, sl), got_faces, got_lines, face_sums, line_sums, own, tiles)
    conv = lax.dot_general(wf[...], cols[...], (((1,), (1,)), ((), ())), preferred_element_type=F32)
    grads = []
    for t in range(tiles):
        live = occ[t : t + 1, :].astype(F32)
        pre = live * conv[:, t * 512 : (t + 1) * 512]
        logistic = 1.0 / (1.0 + jnp.exp(-pre))
        hidden = (pre * logistic).astype(BF16).astype(F32).T
        hidden_rows[t] = hidden.reshape(64, 8, c)
        cut_pieces(hidden.reshape(8, 8, 8, c), t, faces, lines)
        grad = own[t].reshape(512, c).T
        act = (grad * live * logistic * (1.0 + pre * (1.0 - logistic))).astype(BF16)
        grads.append(act)
        conv_back(act.astype(F32).T, wb, wide_back, spread, t, own_out, grad_faces, grad_lines)
    fill_outgoing((sf, sl, vf, vl), out, faces, lines, grad_faces, grad_lines)
    deal_term(jnp.concatenate(grads, axis=1), cols, terms)


def third_kernel(sf, sl, fp, lp, arrived, hidden_rows, own_in, occ, feat, cot, wf,
                 block_out, feature_grad, terms,
                 got_faces, got_lines, face_sums, line_sums, block, wide, cols, own):
    tiles, c = feat.shape[0], feat.shape[1]
    fcap, lcap = sf.shape[1], sl.shape[1]
    wide[:, :, :, 3 * c :] = jnp.zeros((10, 10, 8, c), F32)
    unpack(arrived, got_faces, got_lines, fcap, lcap)
    grads = []
    for t in range(tiles):
        own[t] = own_in[t].reshape(8, 8, 8, c)
        build_columns(hidden_rows[t].reshape(8, 8, 8, c), t, fp, lp, got_faces, got_lines, block, wide, cols)
        grads.append((cot[t].astype(F32) * occ[t : t + 1, :].astype(F32)).astype(BF16))
    deal_term(jnp.concatenate(grads, axis=1), cols, terms)
    conv = lax.dot_general(wf[...], cols[...], (((1,), (1,)), ((), ())), preferred_element_type=F32)
    fold_pieces((sf, sl), got_faces, got_lines, face_sums, line_sums, own, tiles)
    for t in range(tiles):
        live = occ[t : t + 1, :].astype(F32)
        branch = live * conv[:, t * 512 : (t + 1) * 512]
        block_out[t] = (feat[t].astype(F32) * live + branch).astype(BF16)
        sums = own[t].reshape(512, c).T
        feature_grad[t] = ((cot[t].astype(F32) + sums) * live).astype(BF16)


def forward_weight(weight):
    c = weight.shape[1]
    flat = weight.reshape(9, 3, c, c).transpose(2, 0, 1, 3)
    return jnp.pad(flat, ((0, 0), (0, 0), (0, 1), (0, 0))).reshape(c, 36 * c)


def back_weight(weight):
    c = weight.shape[1]
    flat = weight.reshape(3, 3, 3, c, c).transpose(0, 1, 3, 2, 4)
    flat = jnp.pad(flat, ((0, 0), (0, 1), (0, 0), (0, 0), (0, 0)))
    return flat.reshape(12 * c, 3 * c)


def trade(outgoing):
    return lax.all_to_all(outgoing, OWNER_AXES, split_axis=0, concat_axis=0, tiled=True)


def plan(owner, want, owners, cap):
    count = owner.shape[0]
    at = jnp.arange(count, dtype=jnp.int32)
    earlier = (at[None, :] < at[:, None]) & (owner[None, :] == owner[:, None])
    pos = owner * cap + jnp.sum(earlier.astype(jnp.int32), axis=1)
    hit = pos[None, :] == jnp.arange(owners * cap, dtype=jnp.int32)[:, None]
    ask = jnp.sum(jnp.where(hit, want[None, :], 0), axis=1).reshape(owners, cap)
    inverse = (count - jnp.sum(jnp.where(hit, count - at[None, :], 0), axis=1)).reshape(owners, cap)
    return pos, ask, inverse


def body(features, occupancy, face_owner, face_slot, line_owner, line_slot, weight_one, weight_two, cotangent):
    owners = lax.axis_size(OWNER_AXES)
    tiles, c = features.shape[0], features.shape[1]
    fcap = max(2, 30 * tiles // (4 * owners) + 1)
    lcap = max(2, 100 * tiles // (4 * owners) + 1)
    share = -(-27 // owners)
    height = fcap * 64 + lcap * 8
    opposite = jnp.array(OPPOSITE, jnp.int32)
    need = jnp.array(line_need(), jnp.int32)
    face_pos, face_ask, inv_face = plan(
        face_owner.reshape(-1), (face_slot * 6 + opposite[None, :]).reshape(-1), owners, fcap)
    line_pos, line_ask, inv_line = plan(
        line_owner.reshape(-1), (line_slot * 12 + need[None, :]).reshape(-1), owners, lcap)
    requested = trade(jnp.concatenate([face_ask, line_ask], axis=1))
    served_face, served_line = requested[:, :fcap], requested[:, fcap:]

    wf1, wf2 = forward_weight(weight_one), forward_weight(weight_two)
    wb1, wb2 = back_weight(weight_one), back_weight(weight_two)
    smem = pl.BlockSpec(memory_space=pltpu.SMEM)
    vmem = pl.BlockSpec(memory_space=pltpu.VMEM)
    params = pltpu.CompilerParams(vmem_limit_bytes=56 * 1024 * 1024)
    shape = jax.ShapeDtypeStruct
    table_scratch = [
        pltpu.VMEM((tiles * 6, 8, 8, c), F32),
        pltpu.VMEM((tiles * 12, 8, c), F32),
        pltpu.VMEM((tiles * 6 + 1, 8, 8, c), F32),
        pltpu.VMEM((tiles * 20 + 1, 8, c), F32),
        pltpu.VMEM((12, 10, 8, 4 * c), F32),
        pltpu.VMEM((10, 10, 24, c), F32),
    ]
    got_scratch = [
        pltpu.VMEM((owners * fcap, 8, 8, 2 * c), F32),
        pltpu.VMEM((owners * lcap, 8, 2 * c), F32),
        pltpu.VMEM((tiles * 6, 8, 8, 2 * c), F32),
        pltpu.VMEM((tiles * 12, 8, 2 * c), F32),
        pltpu.VMEM((10, 10, 24, c), F32),
        pltpu.VMEM((10, 10, 8, 4 * c), F32),
        pltpu.VMEM((tiles * 512, 36 * c), BF16),
        pltpu.VMEM((tiles, 8, 8, 8, c), F32),
    ]
    out_block = shape((owners, height, 2 * c), BF16)
    row_block = shape((tiles, 64, 8, c), F32)
    term_block = shape((owners, c, share * c), BF16)
    volume = shape(features.shape, BF16)

    outgoing, rows, hidden_own = pl.pallas_call(
        first_kernel,
        out_shape=(out_block, row_block, row_block),
        in_specs=[smem] * 4 + [vmem] * 4,
        out_specs=(vmem,) * 3,
        scratch_shapes=table_scratch,
        compiler_params=params,
    )(served_face, served_line, inv_face, inv_line, features, occupancy, cotangent, wb2)
    arrived = trade(outgoing)
    outgoing, hidden_rows, feature_own, first_term = pl.pallas_call(
        second_kernel,
        out_shape=(out_block, row_block, row_block, term_block),
        in_specs=[smem] * 6 + [vmem] * 6,
        out_specs=(vmem,) * 4,
        scratch_shapes=table_scratch + got_scratch,
        compiler_params=params,
    )(served_face, served_line, inv_face, inv_line, face_pos, line_pos,
      arrived, rows, hidden_own, occupancy, wf1, wb1)
    arrived = trade(outgoing)
    first_parts = trade(first_term)
    block_out, feature_grad, second_term = pl.pallas_call(
        third_kernel,
        out_shape=(volume, volume, term_block),
        in_specs=[smem] * 4 + [vmem] * 7,
        out_specs=(vmem,) * 3,
        scratch_shapes=got_scratch,
        compiler_params=params,
    )(served_face, served_line, face_pos, line_pos,
      arrived, hidden_rows, feature_own, occupancy, features, cotangent, wf2)
    second_parts = trade(second_term)
    grad_scale = 1.0 / math.sqrt(512.0 * tiles * owners)

    def finish(parts):
        total = (grad_scale * jnp.sum(parts.astype(F32), axis=0)).astype(BF16)
        gathered = trade(jnp.broadcast_to(total[None], (owners,) + total.shape))
        dealt = gathered.reshape(owners, c, share, c).transpose(0, 2, 1, 3).reshape(owners * share, c, c)
        first = dealt[:18].reshape(9, 2, c, c)
        last = dealt[18:27].reshape(9, 1, c, c)
        return jnp.concatenate([first, last], axis=1).reshape(27, c, c).astype(F32)

    return (block_out, feature_grad, finish(first_parts), finish(second_parts))


def solution(mesh):
    split = P(("scene", "space", "sub"), None, None)
    split2 = P(("scene", "space", "sub"), None)
    in_specs = (split, split2, split, split2, split, split2, P(), P(), split)
    out_specs = (split, split, P("scene", None, None), P("scene", None, None))
    return jax.shard_map(body, mesh=mesh, in_specs=in_specs, out_specs=out_specs, check_vma=False)
```

profile of v0, /device:TPU:0, one launch (start us, length us, event | category | flops | bytes accessed | tf_op | source)
XLA Modules:
  0.0 139.9 jit_solution(792858734199604796)
XLA Ops:
  1.3 0.7 reduce.7
  6.6 0.7 pad_add_fusion
  7.3 7.4 %all-to-all-start = ((s32[16,1,6]{2,1,0:T(1,128)}), s32[16,1,6]{2,1,0:T(1,128)S(1)}, u32[]{:S(2)}, u32[]{:S(2)}) async-start(s32[16,1,6]{2,1,0:T(1,128)} %bitcast.18), calls=%async_computation | async-start | bytes 16384 | tf_op jit(solution)/shard_map/all_to_all | solution.py:307
  14.7 0.7 sub.42.vf
  15.4 0.7 sub.47.vl
  16.1 1.6 %copy.47 = bf16[3,3,3,64,64]{3,1,0,4,2:T(4,128)(2,1)S(1)} copy(bf16[3,3,3,64,64]{4,3,2,1,0:T(8,128)(2,1)} %bitcast.43) | data formatting | bytes 442368 | tf_op jit(solution)/shard_map/reshape | solution.py:301
  18.4 0.9 copy.48.wb
  19.3 1.7 %all-to-all-done = s32[16,1,6]{2,1,0:T(1,128)S(1)} async-done(((s32[16,1,6]{2,1,0:T(1,128)}), s32[16,1,6]{2,1,0:T(1,128)S(1)}, u32[]{:S(2)}, u32[]{:S(2)}) %all-to-all-start) | async-done | bytes 416 | tf_op jit(solution)/shard_map/all_to_all | solution.py:307
  21.0 0.7 slice.43.sl
  21.7 5.2 %shard_map.138 = (bf16[16,160,128]{2,1,0:T(8,128)(2,1)}, f32[2,64,8,64]{3,2,1,0:T(8,128)}, f32[2,64,8,64]{3,2,1,0:T(8,128)}) custom-call(s32[16,2]{1,0:T(8,128)} %bitcast.50, s32[16,4]{1,0:T(8,128)} %slice.43.sl, s32[16,2]{1,0:T(8,128)} %sub.42.vf, s32[16,4]{1,0:T(8,128)} %sub.47.vl, bf16[2,64,512]{2,1,0:T(8,128)(2,1)} %feat.3, s32[2,512]{1,0:T(2,128)} %occ.5, ...), custom_call_target="tpu_custom_call" | custom-call | tf_op jit(solution)/shard_map/pallas_call | solution.py:366
  26.9 4.4 %all-to-all-start.1 = ((bf16[16,160,128]{2,1,0:T(8,128)(2,1)}), bf16[16,160,128]{2,1,0:T(8,128)(2,1)S(1)}, u32[]{:S(2)}, u32[]{:S(2)}) async-start(bf16[16,160,128]{2,1,0:T(8,128)(2,1)} %get-tuple-element.14), calls=%async_computation.1 | async-start | bytes 1310720 | tf_op jit(solution)/shard_map/all_to_all | solution.py:307
  31.4 0.8 copy.50
  32.9 0.9 copy.51.wb
  34.5 1.1 reshape.133.wf
  35.6 12.4 %all-to-all-done.1.arrived = bf16[16,160,128]{2,1,0:T(8,128)(2,1)S(1)} async-done(((bf16[16,160,128]{2,1,0:T(8,128)(2,1)}), bf16[16,160,128]{2,1,0:T(8,128)(2,1)S(1)}, u32[]{:S(2)}, u32[]{:S(2)}) %all-to-all-start.1) | async-done | bytes 655392 | tf_op jit(solution)/shard_map/all_to_all | solution.py:307
  48.0 0.8 copy-done.1
  48.8 9.5 %shard_map.139 = (bf16[16,160,128]{2,1,0:T(8,128)(2,1)}, f32[2,64,8,64]{3,2,1,0:T(8,128)}, f32[2,64,8,64]{3,2,1,0:T(8,128)}, bf16[16,64,128]{2,1,0:T(8,128)(2,1)}) custom-call(s32[16,2]{1,0:T(8,128)} %bitcast.51, s32[16,4]{1,0:T(8,128)} %slice.43.sl, s32[16,2]{1,0:T(8,128)} %sub.42.vf, s32[16,4]{1,0:T(8,128)} %sub.47.vl, s32[12]{0:T(128)} %copy-done.5, ...), custom_call_target="tpu_custom_call" | custom-call | tf_op jit(solution)/shard_map/pallas_call | solution.py:375
  58.3 14.8 %all_to_all.42 = bf16[16,64,128]{2,1,0:T(8,128)(2,1)S(1)} all-to-all(bf16[16,64,128]{2,1,0:T(8,128)(2,1)} %get-tuple-element.22), channel_id=1, replica_groups=mesh['scene'=2,'space'=8,'sub'=2] {'space','sub'}, dimensions={0} | all-to-all | bytes 524288 | tf_op jit(solution)/shard_map/all_to_all | solution.py:307
  73.1 3.6 %all-to-all-start.2 = ((bf16[16,160,128]{2,1,0:T(8,128)(2,1)}), bf16[16,160,128]{2,1,0:T(8,128)(2,1)S(1)}, u32[]{:S(2)}, u32[]{:S(2)}) async-start(bf16[16,160,128]{2,1,0:T(8,128)(2,1)} %get-tuple-element.17), calls=%async_computation.2 | async-start | bytes 1310720 | tf_op jit(solution)/shard_map/all_to_all | solution.py:307
  76.8 16.5 %all-to-all-done.2.arrived = bf16[16,160,128]{2,1,0:T(8,128)(2,1)S(1)} async-done(((bf16[16,160,128]{2,1,0:T(8,128)(2,1)}), bf16[16,160,128]{2,1,0:T(8,128)(2,1)S(1)}, u32[]{:S(2)}, u32[]{:S(2)}) %all-to-all-start.2) | async-done | bytes 655392 | tf_op jit(solution)/shard_map/all_to_all | solution.py:307
  93.3 0.9 broadcast_in_dim.72
  94.1 4.7 %all-to-all-start.4 = ((bf16[16,64,128]{2,1,0:T(8,128)(2,1)}), bf16[16,64,128]{2,1,0:T(8,128)(2,1)S(1)}, u32[]{:S(2)}, u32[]{:S(2)}) async-start(bf16[16,64,128]{2,1,0:T(8,128)(2,1)} %broadcast_in_dim.72), calls=%async_computation.4 | async-start | bytes 524288 | tf_op jit(solution)/shard_map/all_to_all | solution.py:307
  99.6 1.1 reshape.137.wf
  100.7 7.3 %shard_map.140 = (bf16[2,64,512]{2,1,0:T(8,128)(2,1)}, bf16[2,64,512]{2,1,0:T(8,128)(2,1)}, bf16[16,64,128]{2,1,0:T(8,128)(2,1)}) custom-call(s32[16,2]{1,0:T(8,128)} %bitcast.52, s32[16,4]{1,0:T(8,128)} %slice.43.sl, s32[12]{0:T(128)} %copy-done.5, s32[40]{0:T(128)} %copy-done.6, bf16[16,160,128]{2,1,0:T(8,128)(2,1)} %copy-done, ...), custom_call_target="tpu_custom_call" | custom-call | tf_op jit(solution)/shard_map/pallas_call | solution.py:386
  107.9 1.0 all-to-all-done.4
  108.9 5.0 %all-to-all-start.5 = ((bf16[16,64,128]{2,1,0:T(8,128)(2,1)}), bf16[16,64,128]{2,1,0:T(8,128)(2,1)S(1)}, u32[]{:S(2)}, u32[]{:S(2)}) async-start(bf16[16,64,128]{2,1,0:T(8,128)(2,1)} %get-tuple-element.23), calls=%async_computation.5 | async-start | bytes 524288 | tf_op jit(solution)/shard_map/all_to_all | solution.py:307
  114.3 9.7 %all-to-all-done.5 = bf16[16,64,128]{2,1,0:T(8,128)(2,1)S(1)} async-done(((bf16[16,64,128]{2,1,0:T(8,128)(2,1)}), bf16[16,64,128]{2,1,0:T(8,128)(2,1)S(1)}, u32[]{:S(2)}, u32[]{:S(2)}) %all-to-all-start.5) | async-done | bytes 262176 | tf_op jit(solution)/shard_map/all_to_all | solution.py:307
  124.1 0.8 broadcast_in_dim.73
  124.8 3.5 %all-to-all-start.6 = ((bf16[16,64,128]{2,1,0:T(8,128)(2,1)}), bf16[16,64,128]{2,1,0:T(8,128)(2,1)S(1)}, u32[]{:S(2)}, u32[]{:S(2)}) async-start(bf16[16,64,128]{2,1,0:T(8,128)(2,1)} %broadcast_in_dim.73), calls=%async_computation.6 | async-start | bytes 524288 | tf_op jit(solution)/shard_map/all_to_all | solution.py:307
  128.5 1.0 bitcast_convert_fusion.1
  129.6 8.8 %all-to-all-done.6 = bf16[16,64,128]{2,1,0:T(8,128)(2,1)S(1)} async-done(((bf16[16,64,128]{2,1,0:T(8,128)(2,1)}), bf16[16,64,128]{2,1,0:T(8,128)(2,1)S(1)}, u32[]{:S(2)}, u32[]{:S(2)}) %all-to-all-start.6) | async-done | bytes 262176 | tf_op jit(solution)/shard_map/all_to_all | solution.py:307
  138.8 1.0 bitcast_convert_fusion
  (65 shorter events, 8.9 us)
Async XLA Ops:
  0.6 0.7 copy-start.7
  2.2 0.7 copy-start.8
  2.3 0.7 copy-start.12
  2.9 0.6 copy-start.5
  3.6 0.7 copy-start.9
  5.2 0.7 copy-start.10
  5.2 0.7 copy-start.11
  5.9 0.5 copy-start.6
  7.3 13.7 %all-to-all-start = ((s32[16,1,6]{2,1,0:T(1,128)}), s32[16,1,6]{2,1,0:T(1,128)S(1)}, u32[]{:S(2)}, u32[]{:S(2)}) async-start(s32[16,1,6]{2,1,0:T(1,128)} %bitcast.18), calls=%async_computation | async-start | bytes 16384 | tf_op jit(solution)/shard_map/all_to_all | solution.py:307
  21.0 0.7 copy-start.4
  26.9 4.5 %copy-start.2 = (bf16[27,64,64]{2,1,0:T(8,128)(2,1)S(1)}, bf16[27,64,64]{2,1,0:T(8,128)(2,1)}, u32[]{:S(2)}) copy-start(bf16[27,64,64]{2,1,0:T(8,128)(2,1)} %param.17) | copy-start | bytes 663556
  26.9 21.1 %all-to-all-start.1 = ((bf16[16,160,128]{2,1,0:T(8,128)(2,1)}), bf16[16,160,128]{2,1,0:T(8,128)(2,1)S(1)}, u32[]{:S(2)}, u32[]{:S(2)}) async-start(bf16[16,160,128]{2,1,0:T(8,128)(2,1)} %get-tuple-element.14), calls=%async_computation.1 | async-start | bytes 1310720 | tf_op jit(solution)/shard_map/all_to_all | solution.py:307
  48.0 0.8 copy-start.1
  73.1 20.2 %all-to-all-start.2 = ((bf16[16,160,128]{2,1,0:T(8,128)(2,1)}), bf16[16,160,128]{2,1,0:T(8,128)(2,1)S(1)}, u32[]{:S(2)}, u32[]{:S(2)}) async-start(bf16[16,160,128]{2,1,0:T(8,128)(2,1)} %get-tuple-element.17), calls=%async_computation.2 | async-start | bytes 1310720 | tf_op jit(solution)/shard_map/all_to_all | solution.py:307
  76.8 22.1 %copy-start.3 = (bf16[27,64,64]{2,1,0:T(8,128)(2,1)S(1)}, bf16[27,64,64]{2,1,0:T(8,128)(2,1)}, u32[]{:S(2)}) copy-start(bf16[27,64,64]{2,1,0:T(8,128)(2,1)} %param.18) | copy-start | bytes 663556
  93.3 6.0 %copy-start = (bf16[16,160,128]{2,1,0:T(8,128)(2,1)}, bf16[16,160,128]{2,1,0:T(8,128)(2,1)S(1)}, u32[]{:S(2)}) copy-start(bf16[16,160,128]{2,1,0:T(8,128)(2,1)S(1)} %all-to-all-done.2.arrived) | copy-start | bytes 1966084
  94.1 14.8 %all-to-all-start.4 = ((bf16[16,64,128]{2,1,0:T(8,128)(2,1)}), bf16[16,64,128]{2,1,0:T(8,128)(2,1)S(1)}, u32[]{:S(2)}, u32[]{:S(2)}) async-start(bf16[16,64,128]{2,1,0:T(8,128)(2,1)} %broadcast_in_dim.72), calls=%async_computation.4 | async-start | bytes 524288 | tf_op jit(solution)/shard_map/all_to_all | solution.py:307
  108.9 15.1 %all-to-all-start.5 = ((bf16[16,64,128]{2,1,0:T(8,128)(2,1)}), bf16[16,64,128]{2,1,0:T(8,128)(2,1)S(1)}, u32[]{:S(2)}, u32[]{:S(2)}) async-start(bf16[16,64,128]{2,1,0:T(8,128)(2,1)} %get-tuple-element.23), calls=%async_computation.5 | async-start | bytes 524288 | tf_op jit(solution)/shard_map/all_to_all | solution.py:307
  124.8 13.5 %all-to-all-start.6 = ((bf16[16,64,128]{2,1,0:T(8,128)(2,1)}), bf16[16,64,128]{2,1,0:T(8,128)(2,1)S(1)}, u32[]{:S(2)}, u32[]{:S(2)}) async-start(bf16[16,64,128]{2,1,0:T(8,128)(2,1)} %broadcast_in_dim.73), calls=%async_computation.6 | async-start | bytes 524288 | tf_op jit(solution)/shard_map/all_to_all | solution.py:307
where the time goes:
time: 141 us; the launch traced here: 140 us
  waiting for transfers between devices  50.1 us (36%)
  starting transfers between devices  28.7 us (20%)
  Pallas kernels  22 us (16%)
  local copies, waits for them, and re-layouts  18 us (13%)
  blocking collectives  14.8 us (10%)
  other arithmetic  5.33 us (4%)
    all_to_all x6, waiting for transfers between devices, trade(): lax.all_to_all(outgoing, OWNER_AXES, split_axis=0, concat_axis=0, tiled=T...  50.1 us
    all_to_all x6, starting transfers between devices, trade(): lax.all_to_all(outgoing, OWNER_AXES, split_axis=0, concat_axis=0, tiled=T...  28.7 us
    all_to_all x1, blocking collectives, trade(): lax.all_to_all(outgoing, OWNER_AXES, split_axis=0, concat_axis=0, tiled=T...  14.8 us
    pallas_call x1, Pallas kernels, body(): pl.pallas_call(second_kernel, out_shape=(out_block, row_block, row_block,...  9.46 us
    pallas_call x1, Pallas kernels, body(): pl.pallas_call(third_kernel, out_shape=(volume, volume, term_block), in_s...  7.28 us
    pallas_call x1, Pallas kernels, body(): pl.pallas_call(first_kernel, out_shape=(out_block, row_block, row_block),...  5.22 us
    unnamed x27, local copies, waits for them, and re-layouts  4.37 us
  transfers between devices with their start and end apart: 6, of which 6 were waited for; matrix products, arithmetic and copies ran while one was open for 9% of the time, Pallas kernels for 5%

commit v1 on v0

--- a/solution.py
+++ b/solution.py
@@ -216,7 +216,7 @@
             parts.append(term[:, lane : lane + c])
         while len(parts) < share:
             parts.append(jnp.zeros((c, c), F32))
-        terms[d] = (parts[0] if share == 1 else jnp.concatenate(parts, axis=1)).astype(BF16)
+        terms[d] = (parts[0] if share == 1 else jnp.concatenate(parts, axis=1))
 
 
 def first_kernel(sf, sl, vf, vl, feat, occ, cot, wb, out, rows, own,
@@ -290,6 +290,140 @@
         feature_grad[t] = ((cot[t].astype(F32) + sums) * live).astype(BF16)
 
 
+def remote(src, dst, send, recv, device):
+    return pltpu.make_async_remote_copy(
+        src_ref=src, dst_ref=dst, send_sem=send, recv_sem=recv,
+        device_id=device, device_id_type=pl.DeviceIdType.MESH)
+
+
+def exchange_kernel(outgoing, arrived, send, recv, local):
+    owners = outgoing.shape[0]
+    subs = lax.axis_size("sub")
+    me = lax.axis_index("space") * subs + lax.axis_index("sub")
+
+    def place(i):
+        peer = lax.rem(me + i, owners)
+        return peer, {"space": peer // subs, "sub": lax.rem(peer, subs)}
+
+    barrier = pltpu.get_barrier_semaphore()
+    for i in range(1, owners):
+        pl.semaphore_signal(barrier, inc=1, device_id=place(i)[1], device_id_type=pl.DeviceIdType.MESH)
+    own = pltpu.make_async_copy(outgoing.at[me], arrived.at[me], local)
+    own.start()
+    pl.semaphore_wait(barrier, owners - 1)
+    order = sorted(range(1, owners), key=lambda i: abs(i - owners // 2))
+    copies = []
+    for i in order:
+        peer, device = place(i)
+        copy = remote(outgoing.at[peer], arrived.at[me], send.at[i], recv.at[i], device)
+        copy.start()
+        copies.append(copy)
+    own.wait()
+    for copy in copies:
+        copy.wait()
+
+
+def exchange(outgoing, number):
+    owners = outgoing.shape[0]
+    place = pl.BlockSpec(memory_space=pl.ANY)
+    return pl.pallas_call(
+        exchange_kernel,
+        out_shape=jax.ShapeDtypeStruct(outgoing.shape, outgoing.dtype),
+        in_specs=[place],
+        out_specs=place,
+        scratch_shapes=[
+            pltpu.SemaphoreType.DMA((owners,)),
+            pltpu.SemaphoreType.DMA((owners,)),
+            pltpu.SemaphoreType.DMA,
+        ],
+        compiler_params=pltpu.CompilerParams(collective_id=number, has_side_effects=True),
+    )(outgoing)
+
+
+def reduce_kernel(scale, first, second, first_out, second_out, halves, sums, parts, gathered,
+                  half_send, half_recv, part_send, part_recv, gather_send, gather_recv,
+                  last_send, last_recv):
+    spaces, c = sums.shape[0], sums.shape[2]
+    space, sub = lax.axis_index("space"), lax.axis_index("sub")
+    other = 1 - sub
+    partner = {"space": space, "sub": other}
+
+    def peer(i):
+        at = lax.rem(space + i, spaces)
+        return at, {"space": at, "sub": sub}
+
+    barrier = pltpu.get_barrier_semaphore()
+    pl.semaphore_signal(barrier, inc=1, device_id=partner, device_id_type=pl.DeviceIdType.MESH)
+    for i in range(1, spaces):
+        pl.semaphore_signal(barrier, inc=1, device_id=peer(i)[1], device_id_type=pl.DeviceIdType.MESH)
+    pl.semaphore_wait(barrier, spaces)
+    copies = []
+    for j, term in enumerate((first, second)):
+        copy = remote(term.at[pl.ds(other * spaces, spaces)], halves.at[j],
+                      half_send.at[j], half_recv.at[j], partner)
+        copy.start()
+        copies.append(copy)
+    for copy in copies:
+        copy.wait()
+    for j, term in enumerate((first, second)):
+        for s in range(spaces):
+            sums[s, j] = (term[sub * spaces + s] + halves[j, s]).astype(BF16)
+    order = sorted(range(1, spaces), key=lambda i: abs(i - spaces // 2))
+    copies = []
+    for i in order:
+        at, device = peer(i)
+        copy = remote(sums.at[at], parts.at[space], part_send.at[i], part_recv.at[i], device)
+        copy.start()
+        copies.append(copy)
+    parts[space] = sums[space]
+    for copy in copies:
+        copy.wait()
+    total = parts[0].astype(F32)
+    for s in range(1, spaces):
+        total = total + parts[s].astype(F32)
+    gathered[sub, space] = (total * scale).astype(BF16)
+    copies = []
+    for i in order:
+        at, device = peer(i)
+        copy = remote(gathered.at[sub, space], gathered.at[sub, space],
+                      gather_send.at[i], gather_recv.at[i], device)
+        copy.start()
+        copies.append(copy)
+    for copy in copies:
+        copy.wait()
+    copy = remote(gathered.at[sub], gathered.at[sub], last_send, last_recv, partner)
+    copy.start()
+    copy.wait()
+    share = gathered.shape[4] // c
+    for at, k in enumerate(DEAL):
+        owner, lane = at // share, at % share * c
+        for j, out in enumerate((first_out, second_out)):
+            out[k] = gathered[owner // spaces, owner % spaces, j][:, lane : lane + c].astype(F32)
+
+
+def reduce_terms(first, second, scale, number):
+    subs, spaces = lax.axis_size("sub"), lax.axis_size("space")
+    owners, c, width = first.shape
+    vmem = pl.BlockSpec(memory_space=pltpu.VMEM)
+    dma = pltpu.SemaphoreType.DMA
+    return pl.pallas_call(
+        lambda *refs: reduce_kernel(scale, *refs),
+        out_shape=(jax.ShapeDtypeStruct((27, c, c), F32),) * 2,
+        in_specs=[vmem] * 2,
+        out_specs=(vmem,) * 2,
+        scratch_shapes=[
+            pltpu.VMEM((2, spaces, c, width), F32),
+            pltpu.VMEM((spaces, 2, c, width), BF16),
+            pltpu.VMEM((spaces, 2, c, width), BF16),
+            pltpu.VMEM((subs, spaces, 2, c, width), BF16),
+            dma((2,)), dma((2,)), dma((spaces,)), dma((spaces,)),
+            dma((spaces,)), dma((spaces,)), dma, dma,
+        ],
+        compiler_params=pltpu.CompilerParams(
+            collective_id=number, has_side_effects=True, vmem_limit_bytes=32 * 1024 * 1024),
+    )(first, second)
+
+
 def forward_weight(weight):
     c = weight.shape[1]
     flat = weight.reshape(9, 3, c, c).transpose(2, 0, 1, 3)
@@ -360,7 +494,7 @@
     ]
     out_block = shape((owners, height, 2 * c), BF16)
     row_block = shape((tiles, 64, 8, c), F32)
-    term_block = shape((owners, c, share * c), BF16)
+    term_block = shape((owners, c, share * c), F32)
     volume = shape(features.shape, BF16)
 
     outgoing, rows, hidden_own = pl.pallas_call(
@@ -371,7 +505,7 @@
         scratch_shapes=table_scratch,
         compiler_params=params,
     )(served_face, served_line, inv_face, inv_line, features, occupancy, cotangent, wb2)
-    arrived = trade(outgoing)
+    arrived = exchange(outgoing, 0)
     outgoing, hidden_rows, feature_own, first_term = pl.pallas_call(
         second_kernel,
         out_shape=(out_block, row_block, row_block, term_block),
@@ -381,8 +515,7 @@
         compiler_params=params,
     )(served_face, served_line, inv_face, inv_line, face_pos, line_pos,
       arrived, rows, hidden_own, occupancy, wf1, wb1)
-    arrived = trade(outgoing)
-    first_parts = trade(first_term)
+    arrived = exchange(outgoing, 1)
     block_out, feature_grad, second_term = pl.pallas_call(
         third_kernel,
         out_shape=(volume, volume, term_block),
@@ -392,18 +525,9 @@
         compiler_params=params,
     )(served_face, served_line, face_pos, line_pos,
       arrived, hidden_rows, feature_own, occupancy, features, cotangent, wf2)
-    second_parts = trade(second_term)
     grad_scale = 1.0 / math.sqrt(512.0 * tiles * owners)
-
-    def finish(parts):
-        total = (grad_scale * jnp.sum(parts.astype(F32), axis=0)).astype(BF16)
-        gathered = trade(jnp.broadcast_to(total[None], (owners,) + total.shape))
-        dealt = gathered.reshape(owners, c, share, c).transpose(0, 2, 1, 3).reshape(owners * share, c, c)
-        first = dealt[:18].reshape(9, 2, c, c)
-        last = dealt[18:27].reshape(9, 1, c, c)
-        return jnp.concatenate([first, last], axis=1).reshape(27, c, c).astype(F32)
-
-    return (block_out, feature_grad, finish(first_parts), finish(second_parts))
+    first_grad, second_grad = reduce_terms(first_term, second_term, grad_scale, 2)
+    return (block_out, feature_grad, first_grad, second_grad)
 
 
 def solution(mesh):

time: 141 us -> 111 us (0.79)
  Pallas kernels: 22 us -> 81.5 us
  waiting for transfers between devices: 50.1 us -> 0.01 us
  starting transfers between devices: 28.7 us -> 7.39 us
  blocking collectives: 14.8 us -> 0 us
  other arithmetic: 5.33 us -> 2.59 us
    pallas_call x0 -> x3, Pallas kernels: none -> 59.3 us  [the longest x2 37.3 us: exchange(): pl.pallas_call(exchange_kernel, out_shape=jax.ShapeDtypeStruct(outgoing.s...]
    all_to_all x6 -> x1, waiting for transfers between devices: 50.1 us -> 0.01 us  [trade(): lax.all_to_all(outgoing, OWNER_AXES, split_axis=0, concat_axis=0, tiled=T...]
    all_to_all x6 -> x1, starting transfers between devices: 28.7 us -> 7.39 us  [trade(): lax.all_to_all(outgoing, OWNER_AXES, split_axis=0, concat_axis=0, tiled=T...]
    all_to_all x1 -> x0, blocking collectives: 14.8 us -> none  [trade(): lax.all_to_all(outgoing, OWNER_AXES, split_axis=0, concat_axis=0, tiled=T...]
    unnamed x27 -> x29, local copies, waits for them, and re-layouts: 4.37 us -> 6.46 us
    convert_element_type x4 -> x0, other arithmetic: 2.08 us -> none  [the longest x2 2.07 us: finish(): return jnp.concatenate([first, last], axis=1).reshape(27, c, c).astype(F32)]
    broadcast_in_dim x2 -> x0, local copies, waits for them, and re-layouts: 1.62 us -> none  [finish(): gathered = trade(jnp.broadcast_to(total[None], (owners,) + total.shape))]
  transfers between devices with their start and end apart: 6 -> 1, of which waited for: 6 -> 0; matrix products, arithmetic and copies ran while one was open for 9% -> 10% of each run, Pallas kernels for 5% -> 0%
where the time goes in v1:
time: 111 us; the launch traced here: 110 us
  Pallas kernels  81.5 us (73%)
  local copies, waits for them, and re-layouts  18.1 us (16%)
  starting transfers between devices  7.39 us (7%)
  other arithmetic  2.59 us (2%)
    pallas_call x2, Pallas kernels, exchange(): pl.pallas_call(exchange_kernel, out_shape=jax.ShapeDtypeStruct(outgoing.s...  37.3 us
    pallas_call x1, Pallas kernels, reduce_terms(): pl.pallas_call(lambda *refs: reduce_kernel(scale, *refs), out_shape=(jax....  22 us
    pallas_call x1, Pallas kernels, body(): pl.pallas_call(second_kernel, out_shape=(out_block, row_block, row_block,...  9.56 us
    pallas_call x1, Pallas kernels, body(): pl.pallas_call(third_kernel, out_shape=(volume, volume, term_block), in_s...  7.45 us
    all_to_all x1, starting transfers between devices, trade(): lax.all_to_all(outgoing, OWNER_AXES, split_axis=0, concat_axis=0, tiled=T...  7.39 us
    unnamed x29, local copies, waits for them, and re-layouts  6.46 us
    pallas_call x1, Pallas kernels, body(): pl.pallas_call(first_kernel, out_shape=(out_block, row_block, row_block),...  5.22 us
    reshape x4, local copies, waits for them, and re-layouts, back_weight(): return flat.reshape(12 * c, 3 * c)  2.56 us
  transfers between devices with their start and end apart: 1, of which 0 were waited for; matrix products, arithmetic and copies ran while one was open for 10% of the time, Pallas kernels for 0%

profile of v1, /device:TPU:0, one launch (start us, length us, event | category | flops | bytes accessed | tf_op | source)
XLA Modules:
  0.0 110.4 jit_solution(12991277344053149766)
XLA Ops:
  0.6 0.5 broadcast.55
  1.3 0.7 reduce.7
  2.3 0.7 copy-done.8
  3.0 0.4 copy-done.5
  3.6 0.6 copy-done.9
  4.2 0.7 reduce.6
  5.2 0.7 copy-done.10
  5.9 0.5 copy-done.6
  6.6 0.7 pad_add_fusion
  7.3 7.4 %all-to-all-start = ((s32[16,1,6]{2,1,0:T(1,128)}), s32[16,1,6]{2,1,0:T(1,128)S(1)}, u32[]{:S(2)}, u32[]{:S(2)}) async-start(s32[16,1,6]{2,1,0:T(1,128)} %bitcast.10), calls=%async_computation | async-start | bytes 16384 | tf_op jit(solution)/shard_map/all_to_all | solution.py:441
  14.7 0.7 sub.42.vf
  15.4 0.7 sub.47.vl
  16.1 1.6 %copy.47 = bf16[3,3,3,64,64]{3,1,0,4,2:T(4,128)(2,1)S(1)} copy(bf16[3,3,3,64,64]{4,3,2,1,0:T(8,128)(2,1)} %bitcast.29) | data formatting | bytes 442368 | tf_op jit(solution)/shard_map/reshape | solution.py:435
  18.0 0.4 reshape.93
  18.4 0.9 copy.48.wb
  19.4 0.8 copy.50
  20.5 0.4 reshape.97
  20.9 0.9 copy.51.wb
  21.8 0.4 copy.59
  22.5 1.1 reshape.95.wf
  23.6 0.4 copy.58
  24.3 1.1 reshape.99.wf
  25.4 0.7 slice.9.sl
  26.1 5.2 %shard_map.138 = (bf16[16,160,128]{2,1,0:T(8,128)(2,1)}, f32[2,64,8,64]{3,2,1,0:T(8,128)}, f32[2,64,8,64]{3,2,1,0:T(8,128)}) custom-call(s32[16,2]{1,0:T(8,128)} %bitcast.32, s32[16,4]{1,0:T(8,128)} %slice.9.sl, s32[16,2]{1,0:T(8,128)} %sub.42.vf, s32[16,4]{1,0:T(8,128)} %sub.47.vl, bf16[2,64,512]{2,1,0:T(8,128)(2,1)} %feat.3, s32[2,512]{1,0:T(2,128)} %occ.5, ...), custom_call_target="tpu_custom_call" | custom-call | tf_op jit(solution)/shard_map/pallas_call | solution.py:500
  31.3 19.2 %shard_map.139.arrived = bf16[16,160,128]{2,1,0:T(8,128)(2,1)} custom-call(bf16[16,160,128]{2,1,0:T(8,128)(2,1)} %get-tuple-element.16.outgoing), custom_call_target="tpu_custom_call" | custom-call | tf_op jit(solution)/shard_map/pallas_call | solution.py:329
  50.4 9.6 %shard_map.140 = (bf16[16,160,128]{2,1,0:T(8,128)(2,1)}, f32[2,64,8,64]{3,2,1,0:T(8,128)}, f32[2,64,8,64]{3,2,1,0:T(8,128)}, f32[16,64,128]{2,1,0:T(8,128)}) custom-call(s32[16,2]{1,0:T(8,128)} %bitcast.33, s32[16,4]{1,0:T(8,128)} %slice.9.sl, s32[16,2]{1,0:T(8,128)} %sub.42.vf, s32[16,4]{1,0:T(8,128)} %sub.47.vl, s32[12]{0:T(128)} %copy-done.5, ...), custom_call_target="tpu_custom_call" | custom-call | tf_op jit(solution)/shard_map/pallas_call | solution.py:509
  60.0 18.1 %shard_map.141.arrived = bf16[16,160,128]{2,1,0:T(8,128)(2,1)} custom-call(bf16[16,160,128]{2,1,0:T(8,128)(2,1)} %get-tuple-element.19.outgoing), custom_call_target="tpu_custom_call" | custom-call | tf_op jit(solution)/shard_map/pallas_call | solution.py:329
  78.1 7.5 %shard_map.142 = (bf16[2,64,512]{2,1,0:T(8,128)(2,1)}, bf16[2,64,512]{2,1,0:T(8,128)(2,1)}, f32[16,64,128]{2,1,0:T(8,128)}) custom-call(s32[16,2]{1,0:T(8,128)} %bitcast.34, s32[16,4]{1,0:T(8,128)} %slice.9.sl, s32[12]{0:T(128)} %copy-done.5, s32[40]{0:T(128)} %copy-done.6, bf16[16,160,128]{2,1,0:T(8,128)(2,1)} %shard_map.141.arrived, ...), custom_call_target="tpu_custom_call" | custom-call | tf_op jit(solution)/shard_map/pallas_call | solution.py:519
  85.6 1.0 copy-done.1
  86.6 22.0 %shard_map.143 = (f32[27,64,64]{2,1,0:T(8,128)S(1)}, f32[27,64,64]{2,1,0:T(8,128)S(1)}) custom-call(f32[16,64,128]{2,1,0:T(8,128)S(1)} %copy-done, f32[16,64,128]{2,1,0:T(8,128)S(1)} %copy-done.1), custom_call_target="tpu_custom_call" | custom-call | tf_op jit(solution)/shard_map/pallas_call | solution.py:409
  108.6 0.9 copy.62
  109.5 0.9 copy.63
  (41 shorter events, 2.6 us)
Async XLA Ops:
  0.6 0.7 copy-start.7
  2.2 0.7 copy-start.8
  2.3 0.7 copy-start.12
  2.9 0.5 copy-start.5
  3.5 0.7 copy-start.9
  5.1 0.7 copy-start.10
  5.2 0.7 copy-start.11
  5.8 0.6 copy-start.6
  7.3 18.1 %all-to-all-start = ((s32[16,1,6]{2,1,0:T(1,128)}), s32[16,1,6]{2,1,0:T(1,128)S(1)}, u32[]{:S(2)}, u32[]{:S(2)}) async-start(s32[16,1,6]{2,1,0:T(1,128)} %bitcast.10), calls=%async_computation | async-start | bytes 16384 | tf_op jit(solution)/shard_map/all_to_all | solution.py:441
  18.4 1.0 copy-start.2
  22.5 1.1 copy-start.3
  25.4 0.7 copy-start.4
  78.1 7.5 %copy-start = (f32[16,64,128]{2,1,0:T(8,128)S(1)}, f32[16,64,128]{2,1,0:T(8,128)}, u32[]{:S(2)}) copy-start(f32[16,64,128]{2,1,0:T(8,128)} %get-tuple-element.24.refs_0_) | copy-start | bytes 1572868
  85.6 1.0 copy-start.1

commit v2 on v1

--- a/solution.py
+++ b/solution.py
@@ -95,26 +95,46 @@
         grad_lines[tile * 20 + e] = piece
 
 
-def fill_outgoing(idx, out, faces, lines, grad_faces, grad_lines):
-    served_face, served_line, inv_face, inv_line = idx
-    owners, fcap = served_face.shape
-    lcap = served_line.shape[1]
+def fill_outgoing(asked, code, fcap, out, faces, lines, grad_faces, grad_lines):
+    owners, cap = asked.shape
     c = faces.shape[-1]
+    no_face, no_line = grad_faces.shape[0] - 1, grad_lines.shape[0] - 1
 
     def one(d, carry):
         rows = []
-        for s in range(fcap):
-            fwd = faces[served_face[d, s]].reshape(64, c)
-            back = grad_faces[inv_face[d, s]].reshape(64, c)
-            rows.append(jnp.concatenate([fwd, back], axis=1))
-        for s in range(lcap):
-            fwd = lines[served_line[d, s]]
-            back = grad_lines[inv_line[d, s]]
+        for s in range(cap):
+            want = asked[d, s] & 63
+            number = code[d, s] >> 6
+            if s < fcap:
+                fwd = faces[want].reshape(64, c)
+                back = grad_faces[jnp.where(number > 0, number - 1, no_face)].reshape(64, c)
+            else:
+                fwd = lines[want]
+                back = grad_lines[jnp.where(number > 0, number - 1 - no_face, no_line)]
             rows.append(jnp.concatenate([fwd, back], axis=1))
         out[d] = jnp.concatenate(rows, axis=0).astype(BF16)
         return carry
 
     lax.fori_loop(0, owners, one, 0)
+
+
+def lay_forward(weight, flat):
+    c = weight.shape[1]
+    for kxy in range(9):
+        for kz in range(3):
+            lane = (kxy * 4 + kz) * c
+            flat[:, lane : lane + c] = weight[kxy * 3 + kz]
+        flat[:, (kxy * 4 + 3) * c : (kxy * 4 + 4) * c] = jnp.zeros((c, c), BF16)
+
+
+def lay_back(weight, flat):
+    c = weight.shape[1]
+    for kx in range(3):
+        for ky in range(3):
+            row = (kx * 4 + ky) * c
+            for kz in range(3):
+                flat[row : row + c, kz * c : (kz + 1) * c] = weight[kx * 9 + ky * 3 + kz]
+        flat[(kx * 4 + 3) * c : (kx * 4 + 4) * c, :] = jnp.zeros((c, 3 * c), BF16)
 
 
 def unpack(arrived, got_faces, got_lines, fcap, lcap):
@@ -132,11 +152,13 @@
     lax.fori_loop(0, owners, one, 0)
 
 
-def build_columns(cube, tile, face_pos, line_pos, got_faces, got_lines, block, wide, cols):
+def build_columns(cube, tile, pos, caps, got_faces, got_lines, block, wide, cols):
     c = cube.shape[-1]
+    fcap, lcap, face_count = caps
     block[1:9, 1:9, 8:16, :] = cube
     for f in range(6):
-        piece = got_faces[face_pos[tile * 6 + f]][:, :, :c]
+        at = pos[tile * 6 + f]
+        piece = got_faces[(at >> 8) * fcap + (at & 255)][:, :, :c]
         end = 9 * (f % 2)
         if f // 2 == 0:
             block[end, 1:9, 8:16, :] = piece
@@ -145,7 +167,8 @@
         else:
             block[1:9, 1:9, 7 + end, :] = piece
     for e, vector in enumerate(EXTRA):
-        piece = got_lines[line_pos[tile * 20 + e]][:, :c]
+        at = pos[face_count + tile * 20 + e]
+        piece = got_lines[(at >> 8) * lcap + (at & 255)][:, :c]
         px, py, pz = [9 if d > 0 else 0 for d in vector]
         if vector[2] == 0:
             block[px, py, 8:16, :] = piece
@@ -164,20 +187,19 @@
         cols[tile * 512 : (tile + 1) * 512, kxy * 4 * c : (kxy + 1) * 4 * c] = window
 
 
-def fold_pieces(idx, got_faces, got_lines, face_sums, line_sums, own, tiles):
-    served_face, served_line = idx
-    owners, fcap = served_face.shape
-    lcap = served_line.shape[1]
+def fold_pieces(asked, fcap, got_faces, got_lines, face_sums, line_sums, own, tiles):
+    owners = asked.shape[0]
+    lcap = asked.shape[1] - fcap
     c = own.shape[-1]
     face_sums[...] = jnp.zeros_like(face_sums)
     line_sums[...] = jnp.zeros_like(line_sums)
 
     def one(d, carry):
         for s in range(fcap):
-            to = served_face[d, s]
+            to = asked[d, s] & 63
             face_sums[to] = face_sums[to] + got_faces[d * fcap + s]
         for s in range(lcap):
-            to = served_line[d, s]
+            to = asked[d, fcap + s] & 63
             line_sums[to] = line_sums[to] + got_lines[d * lcap + s]
         return carry
 
@@ -219,9 +241,10 @@
         terms[d] = (parts[0] if share == 1 else jnp.concatenate(parts, axis=1))
 
 
-def first_kernel(sf, sl, vf, vl, feat, occ, cot, wb, out, rows, own,
-                 faces, lines, grad_faces, grad_lines, wide, spread):
+def first_kernel(fcap, asked, code, feat, occ, cot, weight, out, rows, own,
+                 faces, lines, grad_faces, grad_lines, wide, spread, wb):
     tiles, c = feat.shape[0], feat.shape[1]
+    lay_back(weight, wb)
     wide[...] = jnp.zeros_like(wide)
     grad_faces[tiles * 6] = jnp.zeros((8, 8, c), F32)
     grad_lines[tiles * 20] = jnp.zeros((8, c), F32)
@@ -232,15 +255,18 @@
         cut_pieces(masked.reshape(8, 8, 8, c), t, faces, lines)
         upstream = (cot[t].astype(F32) * live).T
         conv_back(upstream, wb, wide, spread, t, own, grad_faces, grad_lines)
-    fill_outgoing((sf, sl, vf, vl), out, faces, lines, grad_faces, grad_lines)
-
-
-def second_kernel(sf, sl, vf, vl, fp, lp, arrived, rows, own_in, occ, wf, wb,
+    fill_outgoing(asked, code, fcap, out, faces, lines, grad_faces, grad_lines)
+
+
+def second_kernel(fcap, asked, code, pos, arrived, rows, own_in, occ, weight,
                   out, hidden_rows, own_out, terms,
-                  faces, lines, grad_faces, grad_lines, wide_back, spread,
-                  got_faces, got_lines, face_sums, line_sums, block, wide, cols, own):
+                  faces, lines, grad_faces, grad_lines, wide_back, spread, wb,
+                  got_faces, got_lines, face_sums, line_sums, block, wide, cols, own, wf):
     tiles, c = rows.shape[0], rows.shape[3]
-    fcap, lcap = sf.shape[1], sl.shape[1]
+    lcap = asked.shape[1] - fcap
+    caps = (fcap, lcap, tiles * 6)
+    lay_back(weight, wb)
+    lay_forward(weight, wf)
     wide_back[...] = jnp.zeros_like(wide_back)
     wide[:, :, :, 3 * c :] = jnp.zeros((10, 10, 8, c), F32)
     grad_faces[tiles * 6] = jnp.zeros((8, 8, c), F32)
@@ -248,8 +274,8 @@
     unpack(arrived, got_faces, got_lines, fcap, lcap)
     for t in range(tiles):
         own[t] = own_in[t].reshape(8, 8, 8, c)
-        build_columns(rows[t].reshape(8, 8, 8, c), t, fp, lp, got_faces, got_lines, block, wide, cols)
-    fold_pieces((sf, sl), got_faces, got_lines, face_sums, line_sums, own, tiles)
+        build_columns(rows[t].reshape(8, 8, 8, c), t, pos, caps, got_faces, got_lines, block, wide, cols)
+    fold_pieces(asked, fcap, got_faces, got_lines, face_sums, line_sums, own, tiles)
     conv = lax.dot_general(wf[...], cols[...], (((1,), (1,)), ((), ())), preferred_element_type=F32)
     grads = []
     for t in range(tiles):
@@ -263,25 +289,27 @@
         act = (grad * live * logistic * (1.0 + pre * (1.0 - logistic))).astype(BF16)
         grads.append(act)
         conv_back(act.astype(F32).T, wb, wide_back, spread, t, own_out, grad_faces, grad_lines)
-    fill_outgoing((sf, sl, vf, vl), out, faces, lines, grad_faces, grad_lines)
+    fill_outgoing(asked, code, fcap, out, faces, lines, grad_faces, grad_lines)
     deal_term(jnp.concatenate(grads, axis=1), cols, terms)
 
 
-def third_kernel(sf, sl, fp, lp, arrived, hidden_rows, own_in, occ, feat, cot, wf,
+def third_kernel(fcap, asked, pos, arrived, hidden_rows, own_in, occ, feat, cot, weight,
                  block_out, feature_grad, terms,
-                 got_faces, got_lines, face_sums, line_sums, block, wide, cols, own):
+                 got_faces, got_lines, face_sums, line_sums, block, wide, cols, own, wf):
     tiles, c = feat.shape[0], feat.shape[1]
-    fcap, lcap = sf.shape[1], sl.shape[1]
+    lcap = asked.shape[1] - fcap
+    caps = (fcap, lcap, tiles * 6)
+    lay_forward(weight, wf)
     wide[:, :, :, 3 * c :] = jnp.zeros((10, 10, 8, c), F32)
     unpack(arrived, got_faces, got_lines, fcap, lcap)
     grads = []
     for t in range(tiles):
         own[t] = own_in[t].reshape(8, 8, 8, c)
-        build_columns(hidden_rows[t].reshape(8, 8, 8, c), t, fp, lp, got_faces, got_lines, block, wide, cols)
+        build_columns(hidden_rows[t].reshape(8, 8, 8, c), t, pos, caps, got_faces, got_lines, block, wide, cols)
         grads.append((cot[t].astype(F32) * occ[t : t + 1, :].astype(F32)).astype(BF16))
     deal_term(jnp.concatenate(grads, axis=1), cols, terms)
     conv = lax.dot_general(wf[...], cols[...], (((1,), (1,)), ((), ())), preferred_element_type=F32)
-    fold_pieces((sf, sl), got_faces, got_lines, face_sums, line_sums, own, tiles)
+    fold_pieces(asked, fcap, got_faces, got_lines, face_sums, line_sums, own, tiles)
     for t in range(tiles):
         live = occ[t : t + 1, :].astype(F32)
         branch = live * conv[:, t * 512 : (t + 1) * 512]
@@ -389,11 +417,22 @@
                       gather_send.at[i], gather_recv.at[i], device)
         copy.start()
         copies.append(copy)
+    lasts = []
+
+    def hand_on(i):
+        at = lax.rem(space - i + spaces, spaces)
+        copy = remote(gathered.at[sub, at], gathered.at[sub, at], last_send.at[i], last_recv.at[i], partner)
+        copy.start()
+        lasts.append(copy)
+
+    hand_on(0)
+    for i, copy in reversed(list(zip(order, copies))):
+        copy.wait_recv()
+        hand_on(i)
     for copy in copies:
+        copy.wait_send()
+    for copy in lasts:
         copy.wait()
-    copy = remote(gathered.at[sub], gathered.at[sub], last_send, last_recv, partner)
-    copy.start()
-    copy.wait()
     share = gathered.shape[4] // c
     for at, k in enumerate(DEAL):
         owner, lane = at // share, at % share * c
@@ -417,39 +456,25 @@
             pltpu.VMEM((spaces, 2, c, width), BF16),
             pltpu.VMEM((subs, spaces, 2, c, width), BF16),
             dma((2,)), dma((2,)), dma((spaces,)), dma((spaces,)),
-            dma((spaces,)), dma((spaces,)), dma, dma,
+            dma((spaces,)), dma((spaces,)), dma((spaces,)), dma((spaces,)),
         ],
         compiler_params=pltpu.CompilerParams(
             collective_id=number, has_side_effects=True, vmem_limit_bytes=32 * 1024 * 1024),
     )(first, second)
 
 
-def forward_weight(weight):
-    c = weight.shape[1]
-    flat = weight.reshape(9, 3, c, c).transpose(2, 0, 1, 3)
-    return jnp.pad(flat, ((0, 0), (0, 0), (0, 1), (0, 0))).reshape(c, 36 * c)
-
-
-def back_weight(weight):
-    c = weight.shape[1]
-    flat = weight.reshape(3, 3, 3, c, c).transpose(0, 1, 3, 2, 4)
-    flat = jnp.pad(flat, ((0, 0), (0, 1), (0, 0), (0, 0), (0, 0)))
-    return flat.reshape(12 * c, 3 * c)
-
-
-def trade(outgoing):
-    return lax.all_to_all(outgoing, OWNER_AXES, split_axis=0, concat_axis=0, tiled=True)
-
-
-def plan(owner, want, owners, cap):
+def plan(owner, want, owners, faces, fcap, lcap):
     count = owner.shape[0]
+    cap = fcap + lcap
     at = jnp.arange(count, dtype=jnp.int32)
-    earlier = (at[None, :] < at[:, None]) & (owner[None, :] == owner[:, None])
-    pos = owner * cap + jnp.sum(earlier.astype(jnp.int32), axis=1)
-    hit = pos[None, :] == jnp.arange(owners * cap, dtype=jnp.int32)[:, None]
-    ask = jnp.sum(jnp.where(hit, want[None, :], 0), axis=1).reshape(owners, cap)
-    inverse = (count - jnp.sum(jnp.where(hit, count - at[None, :], 0), axis=1)).reshape(owners, cap)
-    return pos, ask, inverse
+    line = (at >= faces).astype(jnp.int32)
+    group = owner * 2 + line
+    earlier = (at[None, :] < at[:, None]) & (group[None, :] == group[:, None])
+    rank = jnp.sum(earlier.astype(jnp.int32), axis=1)
+    slot = owner * cap + line * fcap + rank
+    hit = slot[None, :] == jnp.arange(owners * cap, dtype=jnp.int32)[:, None]
+    code = jnp.sum(jnp.where(hit, (at * 64 + 64 + want)[None, :], 0), axis=1)
+    return owner * 256 + rank, code.reshape(owners, cap)
 
 
 def body(features, occupancy, face_owner, face_slot, line_owner, line_slot, weight_one, weight_two, cotangent):
@@ -461,15 +486,13 @@
     height = fcap * 64 + lcap * 8
     opposite = jnp.array(OPPOSITE, jnp.int32)
     need = jnp.array(line_need(), jnp.int32)
-    face_pos, face_ask, inv_face = plan(
-        face_owner.reshape(-1), (face_slot * 6 + opposite[None, :]).reshape(-1), owners, fcap)
-    line_pos, line_ask, inv_line = plan(
-        line_owner.reshape(-1), (line_slot * 12 + need[None, :]).reshape(-1), owners, lcap)
-    requested = trade(jnp.concatenate([face_ask, line_ask], axis=1))
-    served_face, served_line = requested[:, :fcap], requested[:, fcap:]
-
-    wf1, wf2 = forward_weight(weight_one), forward_weight(weight_two)
-    wb1, wb2 = back_weight(weight_one), back_weight(weight_two)
+    owner = jnp.concatenate([face_owner.reshape(-1), line_owner.reshape(-1)])
+    want = jnp.concatenate([
+        (face_slot * 6 + opposite[None, :]).reshape(-1), (line_slot * 12 + need[None, :]).reshape(-1)])
+    pos, code = plan(owner, want, owners, tiles * 6, fcap, lcap)
+    sent = jnp.broadcast_to(jnp.pad(code, ((0, 0), (0, 128 - fcap - lcap)))[:, None, :], (owners, 8, 128))
+    asked = exchange(sent, 3)[:, 0, : fcap + lcap]
+
     smem = pl.BlockSpec(memory_space=pltpu.SMEM)
     vmem = pl.BlockSpec(memory_space=pltpu.VMEM)
     params = pltpu.CompilerParams(vmem_limit_bytes=56 * 1024 * 1024)
@@ -481,6 +504,7 @@
         pltpu.VMEM((tiles * 20 + 1, 8, c), F32),
         pltpu.VMEM((12, 10, 8, 4 * c), F32),
         pltpu.VMEM((10, 10, 24, c), F32),
+        pltpu.VMEM((12 * c, 3 * c), BF16),
     ]
     got_scratch = [
         pltpu.VMEM((owners * fcap, 8, 8, 2 * c), F32),
@@ -491,6 +515,7 @@
         pltpu.VMEM((10, 10, 8, 4 * c), F32),
         pltpu.VMEM((tiles * 512, 36 * c), BF16),
         pltpu.VMEM((tiles, 8, 8, 8, c), F32),
+        pltpu.VMEM((c, 36 * c), BF16),
     ]
     out_block = shape((owners, height, 2 * c), BF16)
     row_block = shape((tiles, 64, 8, c), F32)
@@ -498,33 +523,31 @@
     volume = shape(features.shape, BF16)
 
     outgoing, rows, hidden_own = pl.pallas_call(
-        first_kernel,
+        lambda *refs: first_kernel(fcap, *refs),
         out_shape=(out_block, row_block, row_block),
-        in_specs=[smem] * 4 + [vmem] * 4,
+        in_specs=[smem] * 2 + [vmem] * 4,
         out_specs=(vmem,) * 3,
         scratch_shapes=table_scratch,
         compiler_params=params,
-    )(served_face, served_line, inv_face, inv_line, features, occupancy, cotangent, wb2)
+    )(asked, code, features, occupancy, cotangent, weight_two)
     arrived = exchange(outgoing, 0)
     outgoing, hidden_rows, feature_own, first_term = pl.pallas_call(
-        second_kernel,
+        lambda *refs: second_kernel(fcap, *refs),
         out_shape=(out_block, row_block, row_block, term_block),
-        in_specs=[smem] * 6 + [vmem] * 6,
+        in_specs=[smem] * 3 + [vmem] * 5,
         out_specs=(vmem,) * 4,
         scratch_shapes=table_scratch + got_scratch,
         compiler_params=params,
-    )(served_face, served_line, inv_face, inv_line, face_pos, line_pos,
-      arrived, rows, hidden_own, occupancy, wf1, wb1)
+    )(asked, code, pos, arrived, rows, hidden_own, occupancy, weight_one)
     arrived = exchange(outgoing, 1)
     block_out, feature_grad, second_term = pl.pallas_call(
-        third_kernel,
+        lambda *refs: third_kernel(fcap, *refs),
         out_shape=(volume, volume, term_block),
-        in_specs=[smem] * 4 + [vmem] * 7,
+        in_specs=[smem] * 2 + [vmem] * 7,
         out_specs=(vmem,) * 3,
         scratch_shapes=got_scratch,
         compiler_params=params,
-    )(served_face, served_line, face_pos, line_pos,
-      arrived, hidden_rows, feature_own, occupancy, features, cotangent, wf2)
+    )(asked, pos, arrived, hidden_rows, feature_own, occupancy, features, cotangent, weight_two)
     grad_scale = 1.0 / math.sqrt(512.0 * tiles * owners)
     first_grad, second_grad = reduce_terms(first_term, second_term, grad_scale, 2)
     return (block_out, feature_grad, first_grad, second_grad)

time: 111 us -> 103 us (0.928)
  local copies, waits for them, and re-layouts: 18.1 us -> 8.47 us
  Pallas kernels: 81.5 us -> 90.6 us
  starting transfers between devices: 7.39 us -> 0 us
    pallas_call x2 -> x3, Pallas kernels: 37.3 us -> 46 us  [exchange(): pl.pallas_call(exchange_kernel, out_shape=jax.ShapeDtypeStruct(outgoing.s...]
    reshape x14 -> x1, local copies, waits for them, and re-layouts: 8.23 us -> 0.08 us  [plan(): return (owner * 256 + rank, code.reshape(owners, cap))]
    all_to_all x1 -> x0, starting transfers between devices: 7.39 us -> none  [trade(): lax.all_to_all(outgoing, OWNER_AXES, split_axis=0, concat_axis=0, tiled=T...]
    sub x2 -> x0, local copies, waits for them, and re-layouts: 1.37 us -> none  [plan(): count - jnp.sum(jnp.where(hit, count - at[None, :], 0), axis=1)]
    pad x4 -> x1, local copies, waits for them, and re-layouts: 1.24 us -> 0.01 us  [body(): jnp.pad(code, ((0, 0), (0, 128 - fcap - lcap)))[:, None, :]]
    unnamed x29 -> x19, local copies, waits for them, and re-layouts: 6.46 us -> 5.98 us
  transfers between devices with their start and end apart: 1 -> 0, of which waited for: 0 -> 0; matrix products, arithmetic and copies ran while one was open for 10% -> 0% of each run, Pallas kernels for 0% -> 0%
where the time goes in v2:
time: 103 us
  Pallas kernels  90.6 us (88%)
  local copies, waits for them, and re-layouts  8.47 us (8%)
  other arithmetic  2.97 us (3%)
    pallas_call x3, Pallas kernels, exchange(): pl.pallas_call(exchange_kernel, out_shape=jax.ShapeDtypeStruct(outgoing.s...  46 us
    pallas_call x1, Pallas kernels, reduce_terms(): pl.pallas_call(lambda *refs: reduce_kernel(scale, *refs), out_shape=(jax....  22.1 us
    pallas_call x1, Pallas kernels, body(): pl.pallas_call(lambda *refs: second_kernel(fcap, *refs), out_shape=(out_b...  9.76 us
    pallas_call x1, Pallas kernels, body(): pl.pallas_call(lambda *refs: third_kernel(fcap, *refs), out_shape=(volume...  7.64 us
    unnamed x19, local copies, waits for them, and re-layouts  5.98 us
    pallas_call x1, Pallas kernels, body(): pl.pallas_call(lambda *refs: first_kernel(fcap, *refs), out_shape=(out_bl...  5.17 us

profile of v2, /device:TPU:0, one launch (start us, length us, event | category | flops | bytes accessed | tf_op | source)
XLA Modules:
  0.0 102.8 jit_solution(3544038158625809279)
XLA Ops:
  0.6 0.0 copy-start.6
  0.6 0.6 copy-done.6
  1.3 0.7 multiply_add_fusion.1
  2.0 0.1 concatenate.33
  2.1 0.6 copy-done.3
  2.7 0.1 concatenate.34
  2.7 0.5 broadcast.71
  3.3 0.2 copy-done.4
  3.4 0.7 reduce.7
  4.1 0.1 concatenate.30
  4.2 0.6 copy-done.5
  4.8 0.7 reduce.6
  5.4 0.1 concatenate.31
  5.5 0.1 fusion.3
  5.6 0.2 convert_reduce_fusion
  5.8 0.6 multiply_add_fusion.2
  6.4 0.1 select_reduce_fusion
  6.5 0.1 reshape.110.refs_1_
  6.6 0.0 copy-start.2
  6.6 0.6 copy-done.2
  7.2 0.6 broadcast_in_dim.12.outgoing
  7.8 9.4 %shard_map.138 = s32[16,8,128]{2,1,0:T(8,128)} custom-call(s32[16,8,128]{2,1,0:T(8,128)} %broadcast_in_dim.12.outgoing), custom_call_target="tpu_custom_call" | custom-call | tf_op jit(solution)/shard_map/pallas_call | solution.py:357
  17.2 1.4 %slice.3 = s32[16,1,6]{2,1,0:T(1,128)} slice(s32[16,8,128]{2,1,0:T(8,128)} %shard_map.138), slice={[0:16], [0:1], [0:6]} | slice | bytes 768 | tf_op jit(solution)/shard_map/slice | solution.py:494
  18.6 5.2 %shard_map.139 = (bf16[16,160,128]{2,1,0:T(8,128)(2,1)}, f32[2,64,8,64]{3,2,1,0:T(8,128)}, f32[2,64,8,64]{3,2,1,0:T(8,128)}) custom-call(s32[16,6]{1,0:T(8,128)} %bitcast.3, s32[16,6]{1,0:T(8,128)} %copy-done.2, bf16[2,64,512]{2,1,0:T(8,128)(2,1)} %refs_6_.3, s32[2,512]{1,0:T(2,128)} %refs_5_.3, bf16[2,64,512]{2,1,0:T(8,128)(2,1)} %refs_7_.3, ...), custom_call_target="tpu_custom_call" | custom-call | tf_op jit(solution)/shard_map/pallas_call | solution.py:525
  23.8 18.2 %shard_map.140.refs_3_ = bf16[16,160,128]{2,1,0:T(8,128)(2,1)} custom-call(bf16[16,160,128]{2,1,0:T(8,128)(2,1)} %get-tuple-element.16.outgoing), custom_call_target="tpu_custom_call" | custom-call | tf_op jit(solution)/shard_map/pallas_call | solution.py:357
  42.0 9.8 %shard_map.141 = (bf16[16,160,128]{2,1,0:T(8,128)(2,1)}, f32[2,64,8,64]{3,2,1,0:T(8,128)}, f32[2,64,8,64]{3,2,1,0:T(8,128)}, f32[16,64,128]{2,1,0:T(8,128)}) custom-call(s32[16,6]{1,0:T(8,128)} %bitcast.4, s32[16,6]{1,0:T(8,128)} %copy-done.2, s32[52]{0:T(128)} %get-tuple-element.28.refs_2_.refs_1_, bf16[16,160,128]{2,1,0:T(8,128)(2,1)} %shard_map.140.refs_3_, ...), custom_call_target="tpu_custom_call" | custom-call | tf_op jit(solution)/shard_map/pallas_call | solution.py:534
  51.8 18.4 %shard_map.142.refs_2_ = bf16[16,160,128]{2,1,0:T(8,128)(2,1)} custom-call(bf16[16,160,128]{2,1,0:T(8,128)(2,1)} %get-tuple-element.19.outgoing), custom_call_target="tpu_custom_call" | custom-call | tf_op jit(solution)/shard_map/pallas_call | solution.py:357
  70.2 7.6 %shard_map.143 = (bf16[2,64,512]{2,1,0:T(8,128)(2,1)}, bf16[2,64,512]{2,1,0:T(8,128)(2,1)}, f32[16,64,128]{2,1,0:T(8,128)}) custom-call(s32[16,6]{1,0:T(8,128)} %bitcast.5, s32[52]{0:T(128)} %get-tuple-element.28.refs_2_.refs_1_, bf16[16,160,128]{2,1,0:T(8,128)(2,1)} %shard_map.142.refs_2_, f32[2,64,8,64]{3,2,1,0:T(8,128)} %get-tuple-element.20.refs_3_, ...), custom_call_target="tpu_custom_call" | custom-call | tf_op jit(solution)/shard_map/pallas_call | solution.py:543
  77.8 1.0 %copy-done.1 = f32[16,64,128]{2,1,0:T(8,128)S(1)} copy-done((f32[16,64,128]{2,1,0:T(8,128)S(1)}, f32[16,64,128]{2,1,0:T(8,128)}, u32[]{:S(2)}) %copy-start.1) | copy-done | bytes 524312
  78.9 22.1 %shard_map.144 = (f32[27,64,64]{2,1,0:T(8,128)S(1)}, f32[27,64,64]{2,1,0:T(8,128)S(1)}) custom-call(f32[16,64,128]{2,1,0:T(8,128)S(1)} %copy-done, f32[16,64,128]{2,1,0:T(8,128)S(1)} %copy-done.1), custom_call_target="tpu_custom_call" | custom-call | tf_op jit(solution)/shard_map/pallas_call | solution.py:448
  101.0 0.9 copy.30
  101.9 0.9 copy.31
  (10 shorter events, 0.0 us)
Async XLA Ops:
  0.6 0.7 copy-start.6
  2.0 0.7 copy-start.3
  2.0 0.7 copy-start.7
  2.7 0.7 copy-start.4
  4.1 0.7 copy-start.5
  6.6 0.6 copy-start.2
  70.2 7.7 %copy-start = (f32[16,64,128]{2,1,0:T(8,128)S(1)}, f32[16,64,128]{2,1,0:T(8,128)}, u32[]{:S(2)}) copy-start(f32[16,64,128]{2,1,0:T(8,128)} %get-tuple-element.24.refs_0_) | copy-start | bytes 1572868
  77.8 1.0 %copy-start.1 = (f32[16,64,128]{2,1,0:T(8,128)S(1)}, f32[16,64,128]{2,1,0:T(8,128)}, u32[]{:S(2)}) copy-start(f32[16,64,128]{2,1,0:T(8,128)} %get-tuple-element.25.refs_1_) | copy-start | bytes 1572868

commit v3 on v2

--- a/solution.py
+++ b/solution.py
@@ -385,25 +385,29 @@
     for i in range(1, spaces):
         pl.semaphore_signal(barrier, inc=1, device_id=peer(i)[1], device_id_type=pl.DeviceIdType.MESH)
     pl.semaphore_wait(barrier, spaces)
+    order = sorted(range(1, spaces), key=lambda i: abs(i - spaces // 2))
+    pieces = []
+    for i in order + [0]:
+        at = lax.rem(space + i, spaces)
+        for j, term in enumerate((first, second)):
+            copy = remote(term.at[other * spaces + at], halves.at[j, at],
+                          half_send.at[j, i], half_recv.at[j, i], partner)
+            copy.start()
+            pieces.append(copy)
     copies = []
-    for j, term in enumerate((first, second)):
-        copy = remote(term.at[pl.ds(other * spaces, spaces)], halves.at[j],
-                      half_send.at[j], half_recv.at[j], partner)
-        copy.start()
-        copies.append(copy)
-    for copy in copies:
-        copy.wait()
-    for j, term in enumerate((first, second)):
-        for s in range(spaces):
-            sums[s, j] = (term[sub * spaces + s] + halves[j, s]).astype(BF16)
-    order = sorted(range(1, spaces), key=lambda i: abs(i - spaces // 2))
-    copies = []
-    for i in order:
+    for turn, i in enumerate(order + [0]):
         at, device = peer(i)
-        copy = remote(sums.at[at], parts.at[space], part_send.at[i], part_recv.at[i], device)
-        copy.start()
-        copies.append(copy)
-    parts[space] = sums[space]
+        for j, term in enumerate((first, second)):
+            pieces[2 * turn + j].wait_recv()
+            sums[at, j] = (term[sub * spaces + at] + halves[j, at]).astype(BF16)
+        if i:
+            copy = remote(sums.at[at], parts.at[space], part_send.at[i], part_recv.at[i], device)
+            copy.start()
+            copies.append(copy)
+        else:
+            parts[space] = sums[at]
+    for copy in pieces:
+        copy.wait_send()
     for copy in copies:
         copy.wait()
     total = parts[0].astype(F32)
@@ -455,7 +459,7 @@
             pltpu.VMEM((spaces, 2, c, width), BF16),
             pltpu.VMEM((spaces, 2, c, width), BF16),
             pltpu.VMEM((subs, spaces, 2, c, width), BF16),
-            dma((2,)), dma((2,)), dma((spaces,)), dma((spaces,)),
+            dma((2, spaces)), dma((2, spaces)), dma((spaces,)), dma((spaces,)),
             dma((spaces,)), dma((spaces,)), dma((spaces,)), dma((spaces,)),
         ],
         compiler_params=pltpu.CompilerParams(

time: 103 us -> 102 us (level)
  no operation moved by 1% of the time
where the time goes in v3:
time: 102 us
  Pallas kernels  89.9 us (88%)
  local copies, waits for them, and re-layouts  8.47 us (8%)
  other arithmetic  2.97 us (3%)
    pallas_call x3, Pallas kernels, exchange(): pl.pallas_call(exchange_kernel, out_shape=jax.ShapeDtypeStruct(outgoing.s...  46 us
    pallas_call x1, Pallas kernels, reduce_terms(): pl.pallas_call(lambda *refs: reduce_kernel(scale, *refs), out_shape=(jax....  21.4 us
    pallas_call x1, Pallas kernels, body(): pl.pallas_call(lambda *refs: second_kernel(fcap, *refs), out_shape=(out_b...  9.76 us
    pallas_call x1, Pallas kernels, body(): pl.pallas_call(lambda *refs: third_kernel(fcap, *refs), out_shape=(volume...  7.64 us
    unnamed x19, local copies, waits for them, and re-layouts  5.98 us
    pallas_call x1, Pallas kernels, body(): pl.pallas_call(lambda *refs: first_kernel(fcap, *refs), out_shape=(out_bl...  5.17 us

profile of v3, /device:TPU:0, one launch (start us, length us, event | category | flops | bytes accessed | tf_op | source)
XLA Modules:
  0.0 102.1 jit_solution(13448678485890871806)
XLA Ops:
  0.6 0.0 copy-start.6
  0.6 0.6 copy-done.6
  1.3 0.7 multiply_add_fusion.1
  2.0 0.1 concatenate.33
  2.1 0.6 copy-done.3
  2.7 0.1 concatenate.34
  2.7 0.5 broadcast.71
  3.3 0.2 copy-done.4
  3.4 0.7 reduce.7
  4.1 0.1 concatenate.30
  4.2 0.6 copy-done.5
  4.8 0.7 reduce.6
  5.4 0.1 concatenate.31
  5.5 0.1 fusion.3
  5.6 0.2 convert_reduce_fusion
  5.8 0.6 multiply_add_fusion.2
  6.4 0.1 select_reduce_fusion
  6.5 0.1 reshape.110.refs_1_
  6.6 0.0 copy-start.2
  6.6 0.6 copy-done.2
  7.2 0.6 broadcast_in_dim.12.outgoing
  7.8 9.4 %shard_map.138 = s32[16,8,128]{2,1,0:T(8,128)} custom-call(s32[16,8,128]{2,1,0:T(8,128)} %broadcast_in_dim.12.outgoing), custom_call_target="tpu_custom_call" | custom-call | tf_op jit(solution)/shard_map/pallas_call | solution.py:357
  17.2 1.4 %slice.3 = s32[16,1,6]{2,1,0:T(1,128)} slice(s32[16,8,128]{2,1,0:T(8,128)} %shard_map.138), slice={[0:16], [0:1], [0:6]} | slice | bytes 768 | tf_op jit(solution)/shard_map/slice | solution.py:498
  18.6 5.2 %shard_map.139 = (bf16[16,160,128]{2,1,0:T(8,128)(2,1)}, f32[2,64,8,64]{3,2,1,0:T(8,128)}, f32[2,64,8,64]{3,2,1,0:T(8,128)}) custom-call(s32[16,6]{1,0:T(8,128)} %bitcast.3, s32[16,6]{1,0:T(8,128)} %copy-done.2, bf16[2,64,512]{2,1,0:T(8,128)(2,1)} %refs_6_.3, s32[2,512]{1,0:T(2,128)} %refs_5_.3, bf16[2,64,512]{2,1,0:T(8,128)(2,1)} %refs_7_.3, ...), custom_call_target="tpu_custom_call" | custom-call | tf_op jit(solution)/shard_map/pallas_call | solution.py:529
  23.8 18.2 %shard_map.140.refs_3_ = bf16[16,160,128]{2,1,0:T(8,128)(2,1)} custom-call(bf16[16,160,128]{2,1,0:T(8,128)(2,1)} %get-tuple-element.16.outgoing), custom_call_target="tpu_custom_call" | custom-call | tf_op jit(solution)/shard_map/pallas_call | solution.py:357
  42.0 9.8 %shard_map.141 = (bf16[16,160,128]{2,1,0:T(8,128)(2,1)}, f32[2,64,8,64]{3,2,1,0:T(8,128)}, f32[2,64,8,64]{3,2,1,0:T(8,128)}, f32[16,64,128]{2,1,0:T(8,128)}) custom-call(s32[16,6]{1,0:T(8,128)} %bitcast.4, s32[16,6]{1,0:T(8,128)} %copy-done.2, s32[52]{0:T(128)} %get-tuple-element.28.refs_2_.refs_1_, bf16[16,160,128]{2,1,0:T(8,128)(2,1)} %shard_map.140.refs_3_, ...), custom_call_target="tpu_custom_call" | custom-call | tf_op jit(solution)/shard_map/pallas_call | solution.py:538
  51.8 18.4 %shard_map.142.refs_2_ = bf16[16,160,128]{2,1,0:T(8,128)(2,1)} custom-call(bf16[16,160,128]{2,1,0:T(8,128)(2,1)} %get-tuple-element.19.outgoing), custom_call_target="tpu_custom_call" | custom-call | tf_op jit(solution)/shard_map/pallas_call | solution.py:357
  70.2 7.6 %shard_map.143 = (bf16[2,64,512]{2,1,0:T(8,128)(2,1)}, bf16[2,64,512]{2,1,0:T(8,128)(2,1)}, f32[16,64,128]{2,1,0:T(8,128)}) custom-call(s32[16,6]{1,0:T(8,128)} %bitcast.5, s32[52]{0:T(128)} %get-tuple-element.28.refs_2_.refs_1_, bf16[16,160,128]{2,1,0:T(8,128)(2,1)} %shard_map.142.refs_2_, f32[2,64,8,64]{3,2,1,0:T(8,128)} %get-tuple-element.20.refs_3_, ...), custom_call_target="tpu_custom_call" | custom-call | tf_op jit(solution)/shard_map/pallas_call | solution.py:547
  77.8 1.0 %copy-done.1 = f32[16,64,128]{2,1,0:T(8,128)S(1)} copy-done((f32[16,64,128]{2,1,0:T(8,128)S(1)}, f32[16,64,128]{2,1,0:T(8,128)}, u32[]{:S(2)}) %copy-start.1) | copy-done | bytes 524312
  78.9 21.4 %shard_map.144 = (f32[27,64,64]{2,1,0:T(8,128)S(1)}, f32[27,64,64]{2,1,0:T(8,128)S(1)}) custom-call(f32[16,64,128]{2,1,0:T(8,128)S(1)} %copy-done, f32[16,64,128]{2,1,0:T(8,128)S(1)} %copy-done.1), custom_call_target="tpu_custom_call" | custom-call | tf_op jit(solution)/shard_map/pallas_call | solution.py:452
  100.3 0.9 copy.30
  101.2 0.9 copy.31
  (10 shorter events, 0.0 us)
Async XLA Ops:
  0.6 0.7 copy-start.6
  2.0 0.7 copy-start.3
  2.0 0.7 copy-start.7
  2.7 0.7 copy-start.4
  4.1 0.7 copy-start.5
  6.6 0.6 copy-start.2
  70.2 7.7 %copy-start = (f32[16,64,128]{2,1,0:T(8,128)S(1)}, f32[16,64,128]{2,1,0:T(8,128)}, u32[]{:S(2)}) copy-start(f32[16,64,128]{2,1,0:T(8,128)} %get-tuple-element.24.refs_0_) | copy-start | bytes 1572868
  77.8 1.0 %copy-start.1 = (f32[16,64,128]{2,1,0:T(8,128)S(1)}, f32[16,64,128]{2,1,0:T(8,128)}, u32[]{:S(2)}) copy-start(f32[16,64,128]{2,1,0:T(8,128)} %get-tuple-element.25.refs_1_) | copy-start | bytes 1572868

commit v4 on v3

--- a/solution.py
+++ b/solution.py
@@ -353,7 +353,7 @@
 
 def exchange(outgoing, number):
     owners = outgoing.shape[0]
-    place = pl.BlockSpec(memory_space=pl.ANY)
+    place = pl.BlockSpec(memory_space=pltpu.VMEM)
     return pl.pallas_call(
         exchange_kernel,
         out_shape=jax.ShapeDtypeStruct(outgoing.shape, outgoing.dtype),

time: 102 us -> 107 us (1.049)
  Pallas kernels: 89.9 us -> 94.1 us
    pallas_call x3, Pallas kernels: 46 us -> 50.3 us  [exchange(): pl.pallas_call(exchange_kernel, out_shape=jax.ShapeDtypeStruct(outgoing.s...]
where the time goes in v4:
time: 107 us; the launch traced here: 106 us
  Pallas kernels  94.1 us (88%)
  local copies, waits for them, and re-layouts  8.47 us (8%)
  other arithmetic  2.97 us (3%)
    pallas_call x3, Pallas kernels, exchange(): pl.pallas_call(exchange_kernel, out_shape=jax.ShapeDtypeStruct(outgoing.s...  50.3 us
    pallas_call x1, Pallas kernels, reduce_terms(): pl.pallas_call(lambda *refs: reduce_kernel(scale, *refs), out_shape=(jax....  21.2 us
    pallas_call x1, Pallas kernels, body(): pl.pallas_call(lambda *refs: second_kernel(fcap, *refs), out_shape=(out_b...  9.76 us
    pallas_call x1, Pallas kernels, body(): pl.pallas_call(lambda *refs: third_kernel(fcap, *refs), out_shape=(volume...  7.64 us
    unnamed x19, local copies, waits for them, and re-layouts  5.98 us
    pallas_call x1, Pallas kernels, body(): pl.pallas_call(lambda *refs: first_kernel(fcap, *refs), out_shape=(out_bl...  5.17 us

profile of v4, /device:TPU:0, one launch (start us, length us, event | category | flops | bytes accessed | tf_op | source)
XLA Modules:
  0.0 106.3 jit_solution(154421694516886323)
XLA Ops:
  0.6 0.0 copy-start.6
  0.6 0.6 copy-done.6
  1.3 0.7 multiply_add_fusion.1
  2.0 0.1 concatenate.33
  2.1 0.6 copy-done.3
  2.7 0.1 concatenate.34
  2.7 0.5 broadcast.71
  3.3 0.2 copy-done.4
  3.4 0.7 reduce.7
  4.1 0.1 concatenate.30
  4.2 0.6 copy-done.5
  4.8 0.7 reduce.6
  5.4 0.1 concatenate.31
  5.5 0.1 fusion.3
  5.6 0.2 convert_reduce_fusion
  5.8 0.6 multiply_add_fusion.2
  6.4 0.1 select_reduce_fusion
  6.5 0.1 reshape.110.refs_1_
  6.6 0.0 copy-start.2
  6.6 0.6 copy-done.2
  7.2 0.6 broadcast_in_dim.12.outgoing
  7.8 10.5 %shard_map.138 = s32[16,8,128]{2,1,0:T(8,128)} custom-call(s32[16,8,128]{2,1,0:T(8,128)} %broadcast_in_dim.12.outgoing), custom_call_target="tpu_custom_call" | custom-call | tf_op jit(solution)/shard_map/pallas_call | solution.py:357
  18.3 1.4 %slice.3 = s32[16,1,6]{2,1,0:T(1,128)} slice(s32[16,8,128]{2,1,0:T(8,128)} %shard_map.138), slice={[0:16], [0:1], [0:6]} | slice | bytes 768 | tf_op jit(solution)/shard_map/slice | solution.py:498
  19.8 5.2 %shard_map.139 = (bf16[16,160,128]{2,1,0:T(8,128)(2,1)}, f32[2,64,8,64]{3,2,1,0:T(8,128)}, f32[2,64,8,64]{3,2,1,0:T(8,128)}) custom-call(s32[16,6]{1,0:T(8,128)} %bitcast.3, s32[16,6]{1,0:T(8,128)} %copy-done.2, bf16[2,64,512]{2,1,0:T(8,128)(2,1)} %refs_6_.3, s32[2,512]{1,0:T(2,128)} %refs_5_.3, bf16[2,64,512]{2,1,0:T(8,128)(2,1)} %refs_7_.3, ...), custom_call_target="tpu_custom_call" | custom-call | tf_op jit(solution)/shard_map/pallas_call | solution.py:529
  24.9 19.8 %shard_map.140.refs_3_ = bf16[16,160,128]{2,1,0:T(8,128)(2,1)} custom-call(bf16[16,160,128]{2,1,0:T(8,128)(2,1)} %get-tuple-element.16.outgoing), custom_call_target="tpu_custom_call" | custom-call | tf_op jit(solution)/shard_map/pallas_call | solution.py:357
  44.7 9.8 %shard_map.141 = (bf16[16,160,128]{2,1,0:T(8,128)(2,1)}, f32[2,64,8,64]{3,2,1,0:T(8,128)}, f32[2,64,8,64]{3,2,1,0:T(8,128)}, f32[16,64,128]{2,1,0:T(8,128)}) custom-call(s32[16,6]{1,0:T(8,128)} %bitcast.4, s32[16,6]{1,0:T(8,128)} %copy-done.2, s32[52]{0:T(128)} %get-tuple-element.28.refs_2_.refs_1_, bf16[16,160,128]{2,1,0:T(8,128)(2,1)} %shard_map.140.refs_3_, ...), custom_call_target="tpu_custom_call" | custom-call | tf_op jit(solution)/shard_map/pallas_call | solution.py:538
  54.5 20.0 %shard_map.142.refs_2_ = bf16[16,160,128]{2,1,0:T(8,128)(2,1)} custom-call(bf16[16,160,128]{2,1,0:T(8,128)(2,1)} %get-tuple-element.19.outgoing), custom_call_target="tpu_custom_call" | custom-call | tf_op jit(solution)/shard_map/pallas_call | solution.py:357
  74.5 7.6 %shard_map.143 = (bf16[2,64,512]{2,1,0:T(8,128)(2,1)}, bf16[2,64,512]{2,1,0:T(8,128)(2,1)}, f32[16,64,128]{2,1,0:T(8,128)}) custom-call(s32[16,6]{1,0:T(8,128)} %bitcast.5, s32[52]{0:T(128)} %get-tuple-element.28.refs_2_.refs_1_, bf16[16,160,128]{2,1,0:T(8,128)(2,1)} %shard_map.142.refs_2_, f32[2,64,8,64]{3,2,1,0:T(8,128)} %get-tuple-element.20.refs_3_, ...), custom_call_target="tpu_custom_call" | custom-call | tf_op jit(solution)/shard_map/pallas_call | solution.py:547
  82.2 1.0 copy-done.1
  83.2 21.2 %shard_map.144 = (f32[27,64,64]{2,1,0:T(8,128)S(1)}, f32[27,64,64]{2,1,0:T(8,128)S(1)}) custom-call(f32[16,64,128]{2,1,0:T(8,128)S(1)} %copy-done, f32[16,64,128]{2,1,0:T(8,128)S(1)} %copy-done.1), custom_call_target="tpu_custom_call" | custom-call | tf_op jit(solution)/shard_map/pallas_call | solution.py:452
  104.4 0.9 copy.30
  105.4 0.9 copy.31
  (10 shorter events, 0.0 us)
Async XLA Ops:
  0.6 0.7 copy-start.6
  2.0 0.7 copy-start.3
  2.0 0.7 copy-start.7
  2.7 0.7 copy-start.4
  4.1 0.7 copy-start.5
  6.6 0.6 copy-start.2
  74.5 7.7 %copy-start = (f32[16,64,128]{2,1,0:T(8,128)S(1)}, f32[16,64,128]{2,1,0:T(8,128)}, u32[]{:S(2)}) copy-start(f32[16,64,128]{2,1,0:T(8,128)} %get-tuple-element.24.refs_0_) | copy-start | bytes 1572868
  82.2 1.0 copy-start.1
